TPU v7x, 32 devices: a whole 2x2x4 slice. The times are simulated.
32 devices in a mesh: section: 4 (over x, core), fsdp: 8 (over z, y).
Axes of the slice: x: 2, y: 2, z: 4, core: 2. Of those that a mesh axis runs over, the one named last changes fastest.
Arguments:
- activations: bfloat16 [4, 1024, 4096], P('section', 'fsdp'), may hold values from -6 to 6
- norm_gain: float32 [4, 4096], P('section'), may hold values from 0.1 to 1.9
- trunk_weight: bfloat16 [4, 4096, 4096], P('section', 'fsdp'), may hold values from -0.09375 to 0.09375
- head_weight: bfloat16 [4, 4096, 128], P(None, 'fsdp'), may hold values from -0.09375 to 0.09375
- head_mix: float32 [4, 128, 128], replicated, may hold values from -0.5 to 0.5
- head_steps: int32 [4], replicated, may hold values from 0 to 3, each once
- task_of: int32 [8, 1], replicated, may hold values from 0 to 3
- loss_ratio: float32 [4], replicated, may hold values from 0.5 to 2
- targets: bfloat16 [1024, 128], P('fsdp'), may hold values from -6 to 6
Outputs:
- passed: bfloat16 [4, 1024, 4096], P('section', 'fsdp')
- joined_grad: float32 [4096, 4096], P('fsdp', 'section')
- task_weights: float32 [4], replicated
- task_losses: float32 [4], replicated
Inputs may be any that keep to these rules, and one draw needn't show every extreme that they name: `head_steps`: each value appears once. `task_of`: every task is named by at least one block.
All inputs are finite; a program needn't handle non-finite values.
Results may differ from a plain program's by a relative error of at most 0.017.
Values may be sent and summed in bfloat16 or wider, within the bound.
A program may use at most 64 MiB of HBM per device.

v0:
```python
import jax
import jax.numpy as jnp
from jax import lax
from jax.sharding import PartitionSpec as P

TASKS = 4
OUTS = 128


EPS = 1e-05
ALPHA = 1.5


def partner_2(x, axis, bit):
    return lax.ppermute(x, axis, [(i, i ^ 1 << bit) for i in range(lax.axis_size(axis))])


def shortened(x):
    return jax.tree.map(lambda a: a.astype(jnp.bfloat16) if a.dtype == jnp.float32 else a, x)


def from_behind(x, axis, by):
    devices = lax.axis_size(axis)
    pairs = [(i, i + by) for i in range(devices) if 0 <= i + by < devices]
    return lax.ppermute(x, axis, pairs)


def from_root(block, axis, source):
    block = jnp.where(lax.axis_index(axis) == source, block, jnp.zeros_like(block))
    return lax.psum(block, axis)


def rms_scale(values):
    return values * lax.rsqrt(jnp.mean(values * values, axis=-1, keepdims=True) + EPS)


def head_loss(blocks, head_w, mix_w, step_total, target):
    head_in = rms_scale(blocks).astype(jnp.bfloat16)
    outputs = jnp.dot(head_in, head_w, preferred_element_type=jnp.float32)
    for depth_index in range(TASKS):
        active = (depth_index < step_total).astype(jnp.float32)
        outputs = outputs + active * jnp.tanh(
            jnp.dot(outputs, mix_w, precision=lax.Precision.HIGHEST)
        )
    error_term = outputs - target.astype(jnp.float32)
    return 0.5 * jnp.sum(error_term * error_term)


def pair_concat(own_bit, own_part, other_part, axis_number):
    first = jnp.concatenate([own_part, other_part], axis=axis_number)
    second = jnp.concatenate([other_part, own_part], axis=axis_number)
    return jnp.where(own_bit == 0, first, second)


def finish_weights(norm_sums, loss_sums, counts, loss_ratio):
    grad_norms = jnp.sqrt(norm_sums)
    target_norms = jnp.mean(grad_norms) * loss_ratio**ALPHA
    ratios = target_norms / grad_norms
    task_weights = TASKS * ratios / jnp.sum(ratios)
    return (task_weights, loss_sums / (counts * OUTS))


def local(
    activations,
    norm_gain,
    trunk_weight,
    head_weight,
    head_mix,
    head_steps,
    task_of,
    loss_ratio,
    targets,
):
    fsdp_size = lax.axis_size("fsdp")
    section_size = lax.axis_size("section")
    member = lax.axis_index("fsdp")
    section_index = lax.axis_index("section")
    group_size = min(8, fsdp_size)
    high_count = fsdp_size // group_size
    low_bits = group_size.bit_length() - 1
    high_bits = high_count.bit_length() - 1
    hidden = activations[0]
    row_count, feature_count = hidden.shape
    piece_width = feature_count // fsdp_size
    normed = (rms_scale(hidden.astype(jnp.float32)) * norm_gain[0]).astype(jnp.bfloat16)
    token_block = normed
    for bit_number in range(low_bits):
        partner = partner_2(token_block, "fsdp", bit_number)
        token_block = pair_concat(member >> bit_number & 1, token_block, partner, 0)
    columns = lax.all_to_all(trunk_weight[0], "fsdp", split_axis=1, concat_axis=0, tiled=True)
    for step_index in range(high_bits):
        bit_number = low_bits + step_index
        partner = partner_2(shortened(columns), "fsdp", bit_number).astype(columns.dtype)
        columns = pair_concat(member >> bit_number & 1, columns, partner, 1)
    partial_value = jnp.dot(token_block, columns, preferred_element_type=jnp.float32).astype(
        jnp.bfloat16
    )
    spread = partial_value.reshape(group_size, row_count, 1, high_count, piece_width)
    for bit_number in range(low_bits):
        own_bit = member >> bit_number & 1
        halves = spread.reshape((spread.shape[0] // 2, 2) + spread.shape[1:])
        lower_half = halves[:, 0]
        upper_half = halves[:, 1]
        kept_half = jnp.where(own_bit == 1, upper_half, lower_half)
        sent_half = jnp.where(own_bit == 1, lower_half, upper_half)
        partner = partner_2(sent_half, "fsdp", bit_number)
        spread = pair_concat(own_bit, kept_half, partner, 2)
    pre = spread[0].transpose(0, 2, 1, 3).reshape(row_count, feature_count)
    output = (hidden.astype(jnp.float32) + jax.nn.silu(pre.astype(jnp.float32))).astype(
        jnp.bfloat16
    )
    passed = from_behind(output, "section", 1)
    head_table = lax.all_gather(head_weight, "fsdp", axis=1, tiled=True)
    task_id = task_of[member, 0]
    onehot = (task_of[:, 0][:, None] == jnp.arange(TASKS)[None, :]).astype(jnp.float32)
    counts = row_count * jnp.sum(onehot, axis=0)
    own_task = (jnp.arange(TASKS) == task_id).astype(jnp.float32)
    block_loss, pullback = jax.vjp(
        lambda inner: head_loss(
            inner, head_table[task_id], head_mix[task_id], head_steps[task_id] + 1, targets
        ),
        output.astype(jnp.float32),
    )
    grad_out = pullback(jnp.ones_like(block_loss))[0]
    square = jnp.sum(grad_out * grad_out)
    pre_float = pre.astype(jnp.float32)
    sigmoid_pre = jax.nn.sigmoid(pre_float)
    slope_term = sigmoid_pre * (1.0 + pre_float * (1.0 - sigmoid_pre))
    cotangent = (grad_out * slope_term).astype(jnp.bfloat16)
    last_section = section_size - 1
    normed_all, cotangent_all = (
        from_root(normed, "section", last_section),
        from_root(cotangent, "section", last_section),
    )
    norm_sums, loss_sums = lax.psum((own_task * square, own_task * block_loss), "fsdp")
    task_weights, task_losses = finish_weights(norm_sums, loss_sums, counts, loss_ratio)
    task_weights, task_losses = (
        from_root(task_weights, "section", last_section),
        from_root(task_losses, "section", last_section),
    )
    col_width = feature_count // section_size
    cotangent_cols = lax.dynamic_slice_in_dim(
        cotangent_all, section_index * col_width, col_width, 1
    )
    feature_block = lax.all_to_all(normed_all, "fsdp", split_axis=1, concat_axis=0, tiled=True)
    column_block = lax.all_gather(cotangent_cols, "fsdp", axis=0, tiled=True)
    block_weight = jnp.dot(onehot, task_weights, precision=lax.Precision.HIGHEST)
    per_block = jnp.einsum(
        "btf,btc->bfc",
        feature_block.reshape(fsdp_size, row_count, piece_width),
        column_block.reshape(fsdp_size, row_count, col_width),
        preferred_element_type=jnp.float32,
    )
    joined_grad = jnp.einsum("b,bfc->fc", block_weight, per_block, precision=lax.Precision.HIGHEST)
    return (passed[None], joined_grad, task_weights, task_losses)


def solution(mesh):
    return jax.shard_map(
        local,
        mesh=mesh,
        in_specs=(
            P("section", "fsdp", None),
            P("section", None),
            P("section", "fsdp", None),
            P(None, "fsdp", None),
            P(),
            P(),
            P(),
            P(),
            P("fsdp", None),
        ),
        out_specs=(P("section", "fsdp", None), P("fsdp", "section"), P(), P()),
        check_vma=False,
    )
```

profile of v0, /device:TPU:0, one launch (start us, length us, event | category | flops | bytes accessed | tf_op | source)
XLA Modules:
  0.0 614.6 jit_solution(12914113324198809638)
XLA Ops:
  8.8 2.7 broadcast_select_fusion.2
  11.5 3.0 collective-permute-start
  14.4 6.5 %copy.28 = bf16[1,512,4096]{1,2,0:T(8,128)(2,1)} copy(bf16[1,512,4096]{2,1,0:T(8,128)(2,1)} %param.11) | data formatting | bytes 8388608 | tf_op args[2]
  20.9 4.9 all-to-all-start
  25.8 34.9 %collective-permute-done = bf16[128,4096]{1,0:T(8,128)(2,1)} collective-permute-done((bf16[128,4096]{1,0:T(8,128)(2,1)S(1)}, bf16[128,4096]{1,0:T(8,128)(2,1)}, u32[]{:S(2)}, u32[]{:S(2)}) %collective-permute-start) | collective-permute-done | bytes 1048608 | tf_op jit(solution)/shard_map/ppermute | solution.py:15
  60.7 2.3 maximum_select_fusion.3
  64.4 76.0 %collective-permute-done.1 = bf16[256,4096]{1,0:T(8,128)(2,1)} collective-permute-done((bf16[256,4096]{1,0:T(8,128)(2,1)S(1)}, bf16[256,4096]{1,0:T(8,128)(2,1)}, u32[]{:S(2)}, u32[]{:S(2)}) %collective-permute-start.1) | collective-permute-done | bytes 2097184 | tf_op jit(solution)/shard_map/ppermute | solution.py:15
  140.4 4.9 maximum_select_fusion.2
  145.2 2.4 collective-permute-start.2
  147.9 6.5 %copy.29 = bf16[8,512,512]{2,1,0:T(8,128)(2,1)} copy(bf16[8,512,512]{1,2,0:T(8,128)(2,1)} %bitcast.3) | data formatting | bytes 8388608 | tf_op jit(solution)/shard_map/all_to_all | solution.py:90
  154.4 224.8 %collective-permute-done.2 = bf16[512,4096]{1,0:T(8,128)(2,1)} collective-permute-done((bf16[512,4096]{1,0:T(8,128)(2,1)}, bf16[512,4096]{1,0:T(8,128)(2,1)}, u32[]{:S(2)}, u32[]{:S(2)}) %collective-permute-start.2) | collective-permute-done | bytes 4194336 | tf_op jit(solution)/shard_map/ppermute | solution.py:15
  379.2 9.7 %fusion.20 = bf16[1024,512]{1,0:T(8,128)(2,1)S(1)} fusion(bf16[4096,512]{1,0:T(8,128)(2,1)} %bitcast.112, bf16[512,4096]{1,0:T(8,128)(2,1)} %collective-permute-done.2, bf16[512,4096]{1,0:T(8,128)(2,1)} %maximum_select_fusion.2, pred[]{:T(512)S(6)} %eq.51), kind=kOutput, calls=%fused_computation.36 | convolution fusion | flops 4333240320 | bytes 13631489 | tf_op jit(solution)/shard_map/dot_general | solution.py:95
  390.7 12.2 %collective-permute-done.3 = bf16[4,128,1,1,512]{4,1,0,3,2:T(8,128)(2,1)S(1)} collective-permute-done((bf16[4,128,1,1,512]{4,1,0,3,2:T(8,128)(2,1)S(1)}, bf16[4,128,1,1,512]{4,1,0,3,2:T(8,128)(2,1)S(1)}, u32[]{:S(2)}, u32[]{:S(2)}) %collective-permute-start.3) | collective-permute-done | bytes 524320 | tf_op jit(solution)/shard_map/ppermute | solution.py:15
  403.7 4.6 broadcast_select_fusion
  409.2 13.0 %collective-permute-done.4 = bf16[2,128,2,1,512]{4,2,1,0,3:T(2,128)(2,1)S(1)} collective-permute-done((bf16[2,128,2,1,512]{4,2,1,0,3:T(2,128)(2,1)S(1)}, bf16[2,128,2,1,512]{4,2,1,0,3:T(2,128)(2,1)S(1)}, u32[]{:S(2)}, u32[]{:S(2)}) %collective-permute-start.4) | collective-permute-done | bytes 524320 | tf_op jit(solution)/shard_map/ppermute | solution.py:15
  422.2 1.9 maximum_select_fusion.6
  430.8 17.9 %collective-permute-done.5 = bf16[1,128,4,1,512]{4,2,1,3,0:T(4,128)(2,1)S(1)} collective-permute-done((bf16[1,128,4,1,512]{4,2,1,3,0:T(4,128)(2,1)S(1)}, bf16[1,128,4,1,512]{4,2,1,3,0:T(4,128)(2,1)S(1)}, u32[]{:S(2)}, u32[]{:S(2)}) %collective-permute-start.5) | collective-permute-done | bytes 524320 | tf_op jit(solution)/shard_map/ppermute | solution.py:15
  451.2 1.6 copy.38
  454.2 2.7 fusion.22
  459.5 1.9 fusion.19
  461.4 2.1 broadcast_select_fusion.1
  463.6 50.6 %all-reduce.5.cloned.1.call-done = (bf16[128,4096]{1,0:T(8,128)(2,1)}, bf16[128,8,512]{0,2,1:T(8,128)(2,1)}) async-done(((bf16[128,4096]{1,0:T(8,128)(2,1)}, bf16[128,8,512]{0,2,1:T(8,128)(2,1)}), (bf16[128,4096]{1,0:T(8,128)(2,1)}, bf16[128,8,512]{0,2,1:T(8,128)(2,1)})) %all-reduce.5.cloned.1.call-update) | async-done | bytes 2097168 | tf_op jit(solution)/shard_map/psum | solution.py:30
  514.2 1.7 constant_dynamic-slice_fusion
  515.9 5.5 all-to-all-start.1
  521.4 2.4 collective-permute-start.6
  527.8 34.0 %all-reduce = (f32[4]{0:T(128)S(1)}, f32[4]{0:T(128)S(1)}) all-reduce(f32[4]{0:T(128)S(1)} %compare_select_fusion.1, f32[4]{0:T(128)S(1)} %compare_select_fusion), channel_id=1, replica_groups=mesh['section'=4,'fsdp'=8] {'fsdp'}, use_global_device_ids=true, to_apply=%region_4.5 | all-reduce | flops 8 | bytes 64 | tf_op jit(solution)/shard_map/psum | solution.py:135
  564.4 6.8 %all-reduce.1 = (f32[4]{0:T(128)S(1)}, f32[4]{0:T(128)}) all-reduce(f32[4]{0:T(128)S(1)} %get-tuple-element.31, f32[4]{0:T(128)S(1)} %get-tuple-element.30), channel_id=1, replica_groups=mesh['section'=4,'fsdp'=8] {'section'}, use_global_device_ids=true, to_apply=%region_7.8 | all-reduce | flops 8 | bytes 64 | tf_op jit(solution)/shard_map/psum | solution.py:30
  571.3 6.3 %all-gather.5.cloned.1.call-done = bf16[1024,1024]{1,0:T(8,128)(2,1)} async-done(((bf16[128,1024]{1,0:T(8,128)(2,1)}), bf16[1024,1024]{1,0:T(8,128)(2,1)}) %all-gather.5.cloned.1.call-update) | async-done | bytes 2097168 | tf_op jit(solution)/shard_map/all_gather | solution.py:146
  577.6 4.2 fusion.25
  581.9 22.1 %fusion = f32[1,512,1024]{2,0,1:T(1,128)S(1)} fusion(f32[8,1,1]{0,1,2:T(1,128)S(1)} %convolution_bitcast_fusion, f32[8,512,1024]{2,1,0:T(8,128)S(1)} %fusion.25), kind=kOutput, calls=%fused_computation | convolution fusion | flops 50331648 | bytes 18874400 | tf_op jit(solution)/shard_map/b,bfc->fc/dot_general | solution.py:154
  604.0 1.8 copy.42
  605.8 2.3 copy.46
  (65 shorter events, 22.7 us)
Async XLA Ops:
  7.2 449.7 %copy-start = (f32[4,128,128]{2,1,0:T(8,128)S(1)}, f32[4,128,128]{2,1,0:T(8,128)}, u32[]{:S(2)}) copy-start(f32[4,128,128]{2,1,0:T(8,128)} %param.13) | copy-start | bytes 786436
  11.5 49.2 %collective-permute-start = (bf16[128,4096]{1,0:T(8,128)(2,1)S(1)}, bf16[128,4096]{1,0:T(8,128)(2,1)}, u32[]{:S(2)}, u32[]{:S(2)}) collective-permute-start(bf16[128,4096]{1,0:T(8,128)(2,1)S(1)} %get-tuple-element.11), channel_id=1, source_target_pairs={{0,1},{1,0},{2,3},{3,2},{4,5},{5,4},{6,7},{7,6},{8,9},{9,8},{10,11... | collective-permute-start | bytes 3145736 | tf_op jit(solution)/shard_map/ppermute | solution.py:15
  20.9 127.1 %all-to-all-start = ((bf16[512,8,512]{0,2,1:T(8,128)(2,1)}), bf16[512,8,512]{0,2,1:T(8,128)(2,1)}, u32[]{:S(2)}, u32[]{:S(2)}) async-start(bf16[512,8,512]{0,2,1:T(8,128)(2,1)} %bitcast.110), calls=%async_computation | async-start | bytes 8388608 | tf_op jit(solution)/shard_map/all_to_all | solution.py:90
  25.8 428.4 %all-gather.3.cloned.1.call-start = ((), (), s32[]{:S(2)}) async-start(), calls=%async_computation.2 | async-start | bytes 4718592 | tf_op jit(solution)/shard_map/all_gather | solution.py:113
  62.9 77.4 %collective-permute-start.1 = (bf16[256,4096]{1,0:T(8,128)(2,1)S(1)}, bf16[256,4096]{1,0:T(8,128)(2,1)}, u32[]{:S(2)}, u32[]{:S(2)}) collective-permute-start(bf16[256,4096]{1,0:T(8,128)(2,1)S(1)} %maximum_select_fusion.3), channel_id=1, source_target_pairs={{0,2},{1,3},{2,0},{3,1},{4,6},{5,7},{6,4},{7,5},{8,10},{9,11},{10,... | collective-permute-start | bytes 6291464 | tf_op jit(solution)/shard_map/ppermute | solution.py:15
  145.2 233.9 %collective-permute-start.2 = (bf16[512,4096]{1,0:T(8,128)(2,1)}, bf16[512,4096]{1,0:T(8,128)(2,1)}, u32[]{:S(2)}, u32[]{:S(2)}) collective-permute-start(bf16[512,4096]{1,0:T(8,128)(2,1)} %maximum_select_fusion.2), channel_id=1, source_target_pairs={{0,4},{1,5},{2,6},{3,7},{4,0},{5,1},{6,2},{7,3},{8,12},{9,13},{10,... | collective-permute-start | bytes 12582920 | tf_op jit(solution)/shard_map/ppermute | solution.py:15
  147.7 366.5 %all-reduce.5.cloned.1.call-start = ((), (), s32[]{:S(2)}) async-start(), calls=%async_computation.4 | async-start | bytes 4194304 | tf_op jit(solution)/shard_map/psum | solution.py:30
  389.0 13.9 %collective-permute-start.3 = (bf16[4,128,1,1,512]{4,1,0,3,2:T(8,128)(2,1)S(1)}, bf16[4,128,1,1,512]{4,1,0,3,2:T(8,128)(2,1)S(1)}, u32[]{:S(2)}, u32[]{:S(2)}) collective-permute-start(bf16[4,128,1,1,512]{4,1,0,3,2:T(8,128)(2,1)S(1)} %get-tuple-element.21), channel_id=1, source_target_pairs={{0,1},{1,0},{2,3},{3,2},{4,5},{5,4},{6,7},{7,6},{8,9},{9,8},{10,11... | collective-permute-start | bytes 1572872 | tf_op jit(solution)/shard_map/ppermute | solution.py:15
  409.1 13.1 %collective-permute-start.4 = (bf16[2,128,2,1,512]{4,2,1,0,3:T(2,128)(2,1)S(1)}, bf16[2,128,2,1,512]{4,2,1,0,3:T(2,128)(2,1)S(1)}, u32[]{:S(2)}, u32[]{:S(2)}) collective-permute-start(bf16[2,128,2,1,512]{4,2,1,0,3:T(2,128)(2,1)S(1)} %get-tuple-element.19), channel_id=1, source_target_pairs={{0,2},{1,3},{2,0},{3,1},{4,6},{5,7},{6,4},{7,5},{8,10},{9,11},{10,... | collective-permute-start | bytes 1572872 | tf_op jit(solution)/shard_map/ppermute | solution.py:15
  422.2 3.6 copy-start.8
  422.2 6.1 copy-start.7
  422.2 7.4 %copy-start.4 = (bf16[128,4096]{1,0:T(8,128)(2,1)S(1)}, bf16[128,4096]{1,0:T(8,128)(2,1)}, u32[]{:S(2)}) copy-start(bf16[128,4096]{1,0:T(8,128)(2,1)} %get-tuple-element.10) | copy-start | bytes 3145732
  424.5 24.3 %collective-permute-start.5 = (bf16[1,128,4,1,512]{4,2,1,3,0:T(4,128)(2,1)S(1)}, bf16[1,128,4,1,512]{4,2,1,3,0:T(4,128)(2,1)S(1)}, u32[]{:S(2)}, u32[]{:S(2)}) collective-permute-start(bf16[1,128,4,1,512]{4,2,1,3,0:T(4,128)(2,1)S(1)} %get-tuple-element.17), channel_id=1, source_target_pairs={{0,4},{1,5},{2,6},{3,7},{4,0},{5,1},{6,2},{7,3},{8,12},{9,13},{10,... | collective-permute-start | bytes 1572872 | tf_op jit(solution)/shard_map/ppermute | solution.py:15
  451.2 1.7 copy-start.3
  452.8 1.3 copy-start.1
  454.2 3.4 copy-start.5
  459.5 1.9 copy-start.2
  463.5 114.1 %all-gather.5.cloned.1.call-start = ((), (), s32[]{:S(2)}) async-start(), calls=%async_computation.3 | async-start | bytes 2359296 | tf_op jit(solution)/shard_map/all_gather | solution.py:146
  515.9 55.4 %all-to-all-start.1 = ((bf16[128,8,512]{0,2,1:T(8,128)(2,1)}), bf16[128,8,512]{0,2,1:T(8,128)(2,1)}, u32[]{:S(2)}, u32[]{:S(2)}) async-start(bf16[128,8,512]{0,2,1:T(8,128)(2,1)} %get-tuple-element.9), calls=%async_computation.1 | async-start | bytes 2097152 | tf_op jit(solution)/shard_map/all_to_all | solution.py:145
  521.4 41.7 %copy-start.6 = (f32[4]{0:T(128)S(1)}, f32[4]{0:T(128)}, u32[]{:S(2)}) copy-start(f32[4]{0:T(128)} %param.16) | copy-start | bytes 52
  521.4 49.9 %collective-permute-start.6 = (bf16[128,4096]{1,0:T(8,128)(2,1)S(1)}, bf16[128,4096]{1,0:T(8,128)(2,1)}, u32[]{:S(2)}, u32[]{:S(2)}) collective-permute-start(bf16[128,4096]{1,0:T(8,128)(2,1)S(1)} %get-tuple-element.15), channel_id=1, source_target_pairs={{0,8},{8,16},{16,24},{1,9},{9,17},{17,25},{2,10},{10,18},{18,26},{... | collective-permute-start | bytes 3145736 | tf_op jit(solution)/shard_map/ppermute | solution.py:25
  571.2 10.7 %copy-start.9 = (f32[4]{0:T(128)}, f32[4]{0:T(128)S(1)}, u32[]{:S(2)}) copy-start(f32[4]{0:T(128)S(1)} %get-tuple-element.38) | copy-start | bytes 52
Sparse Core Ops, SparseCore 0:
  147.8 176.0 all-gather.2
  463.7 50.4 all-reduce.4
  517.1 60.4 all-gather.4
where the time goes:
time: 615 us
  waiting for transfers between devices  436 us (71%)
  matrix products  43.4 us (7%)
  blocking collectives  40.8 us (7%)
  other arithmetic  28.2 us (5%)
  local copies, waits for them, and re-layouts  26.4 us (4%)
  starting transfers between devices  22.1 us (4%)
  between operations  18 us (3%)
    ppermute x6, waiting for transfers between devices, partner_2(): lax.ppermute(x, axis, [(i, i ^ 1 << bit) for i in range(lax.axis_size(axi...  379 us
    psum x1, waiting for transfers between devices, from_root(): return lax.psum(block, axis)  50.6 us
    psum x1, blocking collectives, local(): lax.psum((own_task * square, own_task * block_loss), 'fsdp')  34 us
    dot_general x1, matrix products, local(): jnp.einsum('b,bfc->fc', block_weight, per_block, precision=lax.Precision....  22.1 us
    select_n x4, other arithmetic, pair_concat(): return jnp.where(own_bit == 0, first, second)  13.6 us
  transfers between devices with their start and end apart: 12, of which 8 were waited for; matrix products, arithmetic and copies ran while one was open for 8% of the time, Pallas kernels for 0%

commit v1 on v0

v1 whole, which is shorter than its diff:
```python
import jax
import jax.numpy as jnp
from jax import lax
from jax.sharding import PartitionSpec as P

EPS = 1e-05
ALPHA = 1.5
BF = jnp.bfloat16
F32 = jnp.float32


def rms_scale(values):
    return values * lax.rsqrt(jnp.mean(values * values, axis=-1, keepdims=True) + EPS)


def head_loss(blocks, head_w, mix_w, step_total, target, tasks):
    head_in = rms_scale(blocks).astype(BF)
    outputs = jnp.dot(head_in, head_w, preferred_element_type=F32)
    for depth_index in range(tasks):
        active = (depth_index < step_total).astype(F32)
        outputs = outputs + active * jnp.tanh(
            jnp.dot(outputs, mix_w, precision=lax.Precision.HIGHEST)
        )
    error_term = outputs - target.astype(F32)
    return 0.5 * jnp.sum(error_term * error_term)


def line_reduce_scatter(blocks, place, count, inner, stride):
    if count == 1:
        return blocks[0].astype(F32)
    devices = lax.axis_size("fsdp")

    def pairs(step, limit):
        found = []
        for index in range(devices):
            spot = index // stride % count
            if 0 <= spot + step < count and limit(spot):
                found.append((index, index + step * stride))
        return found

    def pick(position):
        return lax.dynamic_index_in_dim(blocks, jnp.clip(position, 0, count - 1), 0, keepdims=False)

    own = pick(place).astype(F32)
    if count == 2:
        swap = pairs(1, lambda s: True) + pairs(-1, lambda s: True)
        return own + lax.ppermute(pick(1 - place).astype(BF), "fsdp", swap).astype(F32)
    right = left = None
    for t in range(1, count):
        send_right = pick(count - t + place)
        send_left = pick(place - count + t)
        if right is not None:
            send_right = send_right.astype(F32) + right.astype(F32)
            send_left = send_left.astype(F32) + left.astype(F32)
        right = lax.ppermute(send_right.astype(BF), "fsdp", pairs(1, lambda s: s <= t - 1))
        left = lax.ppermute(send_left.astype(BF), "fsdp", pairs(-1, lambda s: s >= count - t))
    return own + right.astype(F32) + left.astype(F32)


def spread_pairs(size, bit):
    low = (1 << (bit + 1)) - 1
    return [(i, i ^ (1 << bit)) for i in range(size) if i & low == low]


def local(
    activations,
    norm_gain,
    trunk_weight,
    head_weight,
    head_mix,
    head_steps,
    task_of,
    loss_ratio,
    targets,
):
    fsdp_size = lax.axis_size("fsdp")
    section_size = lax.axis_size("section")
    member = lax.axis_index("fsdp")
    section_index = lax.axis_index("section")
    last_section = section_size - 1
    is_last = section_index == last_section
    section_bits = section_size.bit_length() - 1
    y_size = 1 << ((fsdp_size.bit_length() - 1) // 2)
    z_size = fsdp_size // y_size
    y_place = member % y_size
    z_place = member // y_size
    tasks, head_rows, outs = head_weight.shape

    hidden = activations[0]
    rows, features = hidden.shape
    normed = (rms_scale(hidden.astype(F32)) * norm_gain[0]).astype(BF)
    feature_block = lax.all_to_all(normed, "fsdp", split_axis=1, concat_axis=0, tiled=True)
    weight = trunk_weight[0]

    wanted = head_weight[task_of[:, 0]]
    if head_rows % section_size == 0 and (head_rows // section_size) % 16 == 0:
        share = head_rows // section_size
        part = lax.dynamic_slice_in_dim(wanted, section_index * share, share, 1)
        part = lax.all_to_all(part, "fsdp", split_axis=0, concat_axis=0, tiled=True)
        part = lax.all_gather(part, "section", axis=1, tiled=True)
    else:
        part = lax.all_to_all(wanted, "fsdp", split_axis=0, concat_axis=0, tiled=True)
    head_w = part.reshape(features, outs)

    chunks = 4
    width = features // chunks
    pieces = []
    for c in range(chunks):
        partial = jnp.dot(
            feature_block, weight[:, c * width : (c + 1) * width], preferred_element_type=F32
        ).astype(BF)
        partial = partial.reshape(z_size, y_size, rows, width)
        if c == 1:
            partial = line_reduce_scatter(partial, z_place, z_size, y_size, y_size)
            total = line_reduce_scatter(partial, y_place, y_size, 1, 1)
        else:
            partial = line_reduce_scatter(partial.swapaxes(0, 1), y_place, y_size, 1, 1)
            total = line_reduce_scatter(partial, z_place, z_size, y_size, y_size)
        pieces.append(total.astype(BF))
    pre = jnp.concatenate(pieces, axis=1)
    output = (hidden.astype(F32) + jax.nn.silu(pre.astype(F32))).astype(BF)
    passed = lax.ppermute(output, "section", [(i, i + 1) for i in range(section_size - 1)])

    feature_all = feature_block
    for bit in reversed(range(section_bits)):
        got = lax.ppermute(feature_all, "section", spread_pairs(section_size, bit))
        takes = (section_index >> bit & 1 == 0) & (
            section_index & ((1 << bit) - 1) == (1 << bit) - 1
        )
        feature_all = jnp.where(takes, got, feature_all)

    task_id = task_of[member, 0]
    onehot = (task_of[:, 0][:, None] == jnp.arange(tasks)[None, :]).astype(F32)
    counts = rows * jnp.sum(onehot, axis=0)
    own_task = (jnp.arange(tasks) == task_id).astype(F32)
    block_loss, pullback = jax.vjp(
        lambda inner: head_loss(
            inner, head_w, head_mix[task_id], head_steps[task_id] + 1, targets, tasks
        ),
        output.astype(F32),
    )
    grad_out = pullback(jnp.ones_like(block_loss))[0]
    square = jnp.sum(grad_out * grad_out)
    pre_float = pre.astype(F32)
    sigmoid_pre = jax.nn.sigmoid(pre_float)
    slope_term = sigmoid_pre * (1.0 + pre_float * (1.0 - sigmoid_pre))
    cotangent = (grad_out * slope_term).astype(BF)

    col_width = features // section_size
    cols = cotangent.reshape(rows, section_size, col_width)
    for bit in reversed(range(section_bits)):
        half = cols.reshape(rows, 2, cols.shape[1] // 2, col_width)
        low, high = half[:, 0], half[:, 1]
        got = lax.ppermute(low, "section", spread_pairs(section_size, bit))
        cols = jnp.where(section_index >> bit & 1 == 0, got, high)
    column_block = lax.all_gather(cols[:, 0], "fsdp", axis=0, tiled=True)

    sums = jnp.concatenate([own_task * square, own_task * block_loss])
    sums = lax.psum(jnp.where(is_last, sums, jnp.zeros_like(sums)), ("section", "fsdp"))
    norm_sums, loss_sums = sums[:tasks], sums[tasks:]
    grad_norms = jnp.sqrt(norm_sums)
    ratios = jnp.mean(grad_norms) * loss_ratio**ALPHA / grad_norms
    task_weights = tasks * ratios / jnp.sum(ratios)
    task_losses = loss_sums / (counts * outs)

    block_weight = jnp.sum(onehot * task_weights[None, :], axis=1)
    scaled = (
        column_block.reshape(fsdp_size, rows, col_width).astype(F32)
        * block_weight[:, None, None]
    ).astype(BF)
    joined_grad = lax.dot_general(
        feature_all,
        scaled.reshape(fsdp_size * rows, col_width),
        (((0,), (0,)), ((), ())),
        preferred_element_type=F32,
    )
    return (passed[None], joined_grad, task_weights, task_losses)


def solution(mesh):
    return jax.shard_map(
        local,
        mesh=mesh,
        in_specs=(
            P("section", "fsdp", None),
            P("section", None),
            P("section", "fsdp", None),
            P(None, "fsdp", None),
            P(),
            P(),
            P(),
            P(),
            P("fsdp", None),
        ),
        out_specs=(P("section", "fsdp", None), P("fsdp", "section"), P(), P()),
        check_vma=False,
    )
```

time: 615 us -> 306 us (0.50)
  waiting for transfers between devices: 436 us -> 96.9 us
  starting transfers between devices: 22.1 us -> 97.7 us
  matrix products: 43.4 us -> 16.7 us
  local copies, waits for them, and re-layouts: 26.4 us -> 11.1 us
  other arithmetic: 28.2 us -> 19.8 us
    ppermute x7 -> x33, waiting for transfers between devices: 379 us -> 73.5 us  [the longest x4 44.9 us: line_reduce_scatter(): lax.ppermute(pick(1 - place).astype(BF), 'fsdp', swap).astype(F32)]
    ppermute x7 -> x33, starting transfers between devices: 11.4 us -> 86.2 us  [the longest x12 47 us: line_reduce_scatter(): lax.ppermute(send_right.astype(BF), 'fsdp', pairs(1, lambda s: s <= t - 1))]
    psum x1 -> x0, waiting for transfers between devices: 50.6 us -> none  [from_root(): return lax.psum(block, axis)]
    dot_general x6 -> x7, matrix products: 40.8 us -> 14 us  [the longest x4 6.66 us: local(): jnp.dot(feature_block, weight[:, c * width:(c + 1) * width], preferred_el...]
    all_to_all x2, waiting for transfers between devices: 0.01 us -> 23.3 us  [the longest x1 21.4 us: local(): lax.all_to_all(normed, 'fsdp', split_axis=1, concat_axis=0, tiled=True)]
    select_n x9 -> x4, other arithmetic: 19.5 us -> 2.76 us  [the longest x1 1.15 us: local(): feature_all = jnp.where(takes, got, feature_all)]
    all_to_all x2 -> x0, local copies, waits for them, and re-layouts: 7.78 us -> none  [the longest x1 6.48 us: local(): lax.all_to_all(trunk_weight[0], 'fsdp', split_axis=1, concat_axis=0, tile...]
    all_gather x2, waiting for transfers between devices: 6.3 us -> 0.02 us  [the longest x1 0.02 us: local(): part = lax.all_gather(part, 'section', axis=1, tiled=True)]
  transfers between devices with their start and end apart: 12 -> 37, of which waited for: 8 -> 15; matrix products, arithmetic and copies ran while one was open for 8% -> 8% of each run, Pallas kernels for 0% -> 0%
where the time goes in v1:
time: 306 us; the launch traced here: 305 us
  starting transfers between devices  97.7 us (32%)
  waiting for transfers between devices  96.9 us (32%)
  blocking collectives  44 us (14%)
  other arithmetic  19.8 us (6%)
  between operations  19 us (6%)
  matrix products  16.7 us (5%)
  local copies, waits for them, and re-layouts  11.1 us (4%)
    ppermute x12, starting transfers between devices, line_reduce_scatter(): lax.ppermute(send_right.astype(BF), 'fsdp', pairs(1, lambda s: s <= t - 1))  47 us
    ppermute x4, waiting for transfers between devices, line_reduce_scatter(): lax.ppermute(pick(1 - place).astype(BF), 'fsdp', swap).astype(F32)  44.9 us
    psum x1, blocking collectives, local(): lax.psum(jnp.where(is_last, sums, jnp.zeros_like(sums)), ('section', 'fsd...  44 us
    all_to_all x1, waiting for transfers between devices, local(): lax.all_to_all(normed, 'fsdp', split_axis=1, concat_axis=0, tiled=True)  21.4 us
    ppermute x12, waiting for transfers between devices, line_reduce_scatter(): lax.ppermute(send_right.astype(BF), 'fsdp', pairs(1, lambda s: s <= t - 1))  18.7 us
    ppermute x1, starting transfers between devices, local(): lax.ppermute(output, 'section', [(i, i + 1) for i in range(section_size -...  18.2 us
    ppermute x12, starting transfers between devices, line_reduce_scatter(): lax.ppermute(send_left.astype(BF), 'fsdp', pairs(-1, lambda s: s >= count...  10.8 us
    ppermute x12, waiting for transfers between devices, line_reduce_scatter(): lax.ppermute(send_left.astype(BF), 'fsdp', pairs(-1, lambda s: s >= count...  7.84 us
  transfers between devices with their start and end apart: 37, of which 15 were waited for; matrix products, arithmetic and copies ran while one was open for 8% of the time, Pallas kernels for 0%

profile of v1, /device:TPU:0, one launch (start us, length us, event | category | flops | bytes accessed | tf_op | source)
XLA Modules:
  0.0 305.1 jit_solution(18264459745788927105)
XLA Ops:
  9.7 7.3 %all-to-all-start.1 = ((bf16[8,128,128]{2,1,0:T(8,128)(2,1)}), bf16[8,128,128]{2,1,0:T(8,128)(2,1)S(1)}, u32[]{:S(2)}, u32[]{:S(2)}) async-start(bf16[8,128,128]{2,1,0:T(8,128)(2,1)} %constant_dynamic-slice_fusion.1), calls=%async_computation.1 | async-start | bytes 524288 | tf_op jit(solution)/shard_map/all_to_all | solution.py:99
  17.3 1.7 copy.35
  20.3 3.8 %fusion.22 = bf16[128,8,512]{2,0,1:T(8,128)(2,1)} fusion(f32[128,8,512]{2,1,0:T(8,128)} %bitcast.220, f32[8,512]{1,0:T(8,128)S(1)} %mul.223, f32[128]{0:T(128)S(1)} %add_rsqrt_fusion), kind=kLoop, calls=%fused_computation.38 | loop fusion | flops 1572864 | bytes 3162624 | tf_op jit(solution)/shard_map/convert_element_type | solution.py:91
  24.1 1.8 all-to-all-done.1
  25.9 4.2 %all-to-all-start = ((bf16[128,8,512]{2,0,1:T(8,128)(2,1)}), bf16[128,8,512]{2,0,1:T(8,128)(2,1)S(1)}, u32[]{:S(2)}, u32[]{:S(2)}) async-start(bf16[128,8,512]{2,0,1:T(8,128)(2,1)} %fusion.22), calls=%async_computation | async-start | bytes 2097152 | tf_op jit(solution)/shard_map/all_to_all | solution.py:92
  34.0 21.4 %all-to-all-done = bf16[128,8,512]{2,0,1:T(8,128)(2,1)S(1)} async-done(((bf16[128,8,512]{2,0,1:T(8,128)(2,1)}), bf16[128,8,512]{2,0,1:T(8,128)(2,1)S(1)}, u32[]{:S(2)}, u32[]{:S(2)}) %all-to-all-start) | async-done | bytes 1048608 | tf_op jit(solution)/shard_map/all_to_all | solution.py:92
  55.5 2.9 convolution_convert_fusion.4
  66.7 6.1 %collective-permute-done.7 = bf16[2,128,1024]{2,1,0:T(8,128)(2,1)S(1)} collective-permute-done((bf16[2,128,1024]{2,1,0:T(8,128)(2,1)S(1)}, bf16[2,128,1024]{2,1,0:T(8,128)(2,1)S(1)}, u32[]{:S(2)}, u32[]{:S(2)}) %collective-permute-start.7) | collective-permute-done | bytes 524320 | tf_op jit(solution)/shard_map/ppermute | solution.py:55
  73.0 4.4 %collective-permute-start.8 = (bf16[2,128,1024]{2,1,0:T(8,128)(2,1)S(1)}, bf16[2,128,1024]{2,1,0:T(8,128)(2,1)S(1)}, u32[]{:S(2)}, u32[]{:S(2)}) collective-permute-start(bf16[2,128,1024]{2,1,0:T(8,128)(2,1)S(1)} %fusion.34), channel_id=1, source_target_pairs={{0,2},{1,3},{2,4},{3,5},{8,10},{9,11},{10,12},{11,13},{16,18},{17,... | collective-permute-start | bytes 1572872 | tf_op jit(solution)/shard_map/ppermute | solution.py:55
  77.9 8.0 %collective-permute-done = bf16[4,128,1024]{2,1,0:T(8,128)(2,1)S(1)} collective-permute-done((bf16[4,128,1024]{2,1,0:T(8,128)(2,1)S(1)}, bf16[4,128,1024]{2,1,0:T(8,128)(2,1)S(1)}, u32[]{:S(2)}, u32[]{:S(2)}) %collective-permute-start) | collective-permute-done | bytes 1048608 | tf_op jit(solution)/shard_map/ppermute | solution.py:47
  90.9 17.5 %collective-permute-done.14 = bf16[4,128,1024]{2,1,0:T(8,128)(2,1)S(1)} collective-permute-done((bf16[4,128,1024]{2,1,0:T(8,128)(2,1)S(1)}, bf16[4,128,1024]{2,1,0:T(8,128)(2,1)S(1)}, u32[]{:S(2)}, u32[]{:S(2)}) %collective-permute-start.14) | collective-permute-done | bytes 1048608 | tf_op jit(solution)/shard_map/ppermute | solution.py:47
  110.3 18.1 %collective-permute-done.21 = bf16[4,128,1024]{2,1,0:T(8,128)(2,1)S(1)} collective-permute-done((bf16[4,128,1024]{2,1,0:T(8,128)(2,1)S(1)}, bf16[4,128,1024]{2,1,0:T(8,128)(2,1)S(1)}, u32[]{:S(2)}, u32[]{:S(2)}) %collective-permute-start.21) | collective-permute-done | bytes 1048608 | tf_op jit(solution)/shard_map/ppermute | solution.py:47
  128.3 1.6 collective-permute-start.15
  131.8 4.9 %collective-permute-done.15 = bf16[128,1024]{1,0:T(8,128)(2,1)S(1)} collective-permute-done((bf16[128,1024]{1,0:T(8,128)(2,1)S(1)}, bf16[128,1024]{1,0:T(8,128)(2,1)S(1)}, u32[]{:S(2)}, u32[]{:S(2)}) %collective-permute-start.15) | collective-permute-done | bytes 262176 | tf_op jit(solution)/shard_map/ppermute | solution.py:55
  136.7 4.4 %collective-permute-start.2 = (bf16[128,1024]{1,0:T(8,128)(2,1)S(1)}, bf16[128,1024]{1,0:T(8,128)(2,1)S(1)}, u32[]{:S(2)}, u32[]{:S(2)}) collective-permute-start(bf16[128,1024]{1,0:T(8,128)(2,1)S(1)} %fusion.58), channel_id=1, source_target_pairs={{0,2},{1,3},{2,4},{3,5},{8,10},{9,11},{10,12},{11,13},{16,18},{17,... | collective-permute-start | bytes 786440 | tf_op jit(solution)/shard_map/ppermute | solution.py:55
  145.3 4.4 %collective-permute-start.16 = (bf16[128,1024]{1,0:T(8,128)(2,1)S(1)}, bf16[128,1024]{1,0:T(8,128)(2,1)S(1)}, u32[]{:S(2)}, u32[]{:S(2)}) collective-permute-start(bf16[128,1024]{1,0:T(8,128)(2,1)S(1)} %fusion.51), channel_id=1, source_target_pairs={{0,2},{1,3},{2,4},{3,5},{8,10},{9,11},{10,12},{11,13},{16,18},{17,... | collective-permute-start | bytes 786440 | tf_op jit(solution)/shard_map/ppermute | solution.py:55
  149.9 1.9 collective-permute-start.23
  152.7 3.7 %collective-permute-done.16 = bf16[128,1024]{1,0:T(8,128)(2,1)S(1)} collective-permute-done((bf16[128,1024]{1,0:T(8,128)(2,1)S(1)}, bf16[128,1024]{1,0:T(8,128)(2,1)S(1)}, u32[]{:S(2)}, u32[]{:S(2)}) %collective-permute-start.16) | collective-permute-done | bytes 262176 | tf_op jit(solution)/shard_map/ppermute | solution.py:55
  156.5 4.4 %collective-permute-start.3 = (bf16[128,1024]{1,0:T(8,128)(2,1)S(1)}, bf16[128,1024]{1,0:T(8,128)(2,1)S(1)}, u32[]{:S(2)}, u32[]{:S(2)}) collective-permute-start(bf16[128,1024]{1,0:T(8,128)(2,1)S(1)} %get-tuple-element.12), channel_id=1, source_target_pairs={{0,2},{1,3},{2,4},{3,5},{4,6},{5,7},{8,10},{9,11},{10,12},{11,13},... | collective-permute-start | bytes 786440 | tf_op jit(solution)/shard_map/ppermute | solution.py:55
  164.1 17.8 %collective-permute-start.17 = (bf16[128,1024]{1,0:T(8,128)(2,1)S(1)}, bf16[128,1024]{1,0:T(8,128)(2,1)S(1)}, u32[]{:S(2)}, u32[]{:S(2)}) collective-permute-start(bf16[128,1024]{1,0:T(8,128)(2,1)S(1)} %get-tuple-element.20), channel_id=1, source_target_pairs={{0,2},{1,3},{2,4},{3,5},{4,6},{5,7},{8,10},{9,11},{10,12},{11,13},... | collective-permute-start | bytes 786440 | tf_op jit(solution)/shard_map/ppermute | solution.py:55
  182.0 2.7 collective-permute-start.24
  189.0 5.1 %collective-permute-done.6 = bf16[128,1024]{1,0:T(8,128)(2,1)S(1)} collective-permute-done((bf16[128,1024]{1,0:T(8,128)(2,1)S(1)}, bf16[128,1024]{1,0:T(8,128)(2,1)S(1)}, u32[]{:S(2)}, u32[]{:S(2)}) %collective-permute-start.6) | collective-permute-done | bytes 262176 | tf_op jit(solution)/shard_map/ppermute | solution.py:56
  194.1 2.7 collective-permute-start.13
  197.0 2.7 collective-permute-done.27
  202.2 2.2 fusion.26
  207.6 2.7 multiply_reduce_fusion
  210.4 1.8 reshape_reshape.3
  217.9 2.1 collective-permute-done.32
  220.8 1.7 collective-permute-start.29
  227.0 18.2 %collective-permute-start.28 = (bf16[128,4096]{1,0:T(8,128)(2,1)S(1)}, bf16[128,4096]{1,0:T(8,128)(2,1)S(1)}, u32[]{:S(2)}, u32[]{:S(2)}) collective-permute-start(bf16[128,4096]{1,0:T(8,128)(2,1)S(1)} %get-tuple-element.9), channel_id=1, source_target_pairs={{0,8},{8,16},{16,24},{1,9},{9,17},{17,25},{2,10},{10,18},{18,26},{... | collective-permute-start | bytes 3145736 | tf_op jit(solution)/shard_map/ppermute | solution.py:122
  245.2 44.0 %psum.7 = f32[8]{0:T(128)S(1)} all-reduce(f32[8]{0:T(128)S(1)} %broadcast_select_fusion.1), channel_id=1, replica_groups=mesh['section'=4,'fsdp'=8] {'section','fsdp'}, use_global_device_ids=true, to_apply=%region_5.6 | all-reduce | flops 8 | bytes 64 | tf_op jit(solution)/shard_map/psum | solution.py:159
  292.6 4.7 %fusion.17 = f32[512,1024]{1,0:T(8,128)} fusion(bf16[1024,1,1024]{2,0,1:T(8,128)(2,1)} %all-gather.6.cloned.1.call-done, f32[1024]{0:T(1024)S(1)} %broadcast_bitcast_fusion, bf16[1024,512]{1,0:T(8,128)(2,1)} %collective-permute-done.30, bf16[1024,512]{1,0:T(8,128)(2,1)} %broadcast_select_fusion, pred[]{:T(512)S(6)} %eq.37), kind=kOutput, calls=%fused_computation.29 | convolution fusion | flops 1077411840 | bytes 6295553 | tf_op jit(solution)/shard_map/dot_general | solution.py:171
  (153 shorter events, 55.3 us)
Async XLA Ops:
  9.7 16.2 %all-to-all-start.1 = ((bf16[8,128,128]{2,1,0:T(8,128)(2,1)}), bf16[8,128,128]{2,1,0:T(8,128)(2,1)S(1)}, u32[]{:S(2)}, u32[]{:S(2)}) async-start(bf16[8,128,128]{2,1,0:T(8,128)(2,1)} %constant_dynamic-slice_fusion.1), calls=%async_computation.1 | async-start | bytes 524288 | tf_op jit(solution)/shard_map/all_to_all | solution.py:99
  25.9 29.6 %all-to-all-start = ((bf16[128,8,512]{2,0,1:T(8,128)(2,1)}), bf16[128,8,512]{2,0,1:T(8,128)(2,1)S(1)}, u32[]{:S(2)}, u32[]{:S(2)}) async-start(bf16[128,8,512]{2,0,1:T(8,128)(2,1)} %fusion.22), calls=%async_computation | async-start | bytes 2097152 | tf_op jit(solution)/shard_map/all_to_all | solution.py:92
  30.1 172.1 %all-gather.4.cloned.1.call-start = ((), (), s32[]{:S(2)}) async-start(), calls=%async_computation.2 | async-start | bytes 1310720 | tf_op jit(solution)/shard_map/all_gather | solution.py:100
  34.0 258.6 %all-gather.6.cloned.1.call-start = ((), (), s32[]{:S(2)}) async-start(), calls=%async_computation.3 | async-start | bytes 2359296 | tf_op jit(solution)/shard_map/all_gather | solution.py:156
  59.8 26.2 %collective-permute-start = (bf16[4,128,1024]{2,1,0:T(8,128)(2,1)S(1)}, bf16[4,128,1024]{2,1,0:T(8,128)(2,1)S(1)}, u32[]{:S(2)}, u32[]{:S(2)}) collective-permute-start(bf16[4,128,1024]{2,1,0:T(8,128)(2,1)S(1)} %dynamic-slice_bitcast_fusion.2), channel_id=1, source_target_pairs={{0,1},{2,3},{4,5},{6,7},{1,0},{3,2},{5,4},{7,6},{8,9},{10,11},{12,... | collective-permute-start | bytes 3145736 | tf_op jit(solution)/shard_map/ppermute | solution.py:47
  61.1 11.7 %collective-permute-start.7 = (bf16[2,128,1024]{2,1,0:T(8,128)(2,1)S(1)}, bf16[2,128,1024]{2,1,0:T(8,128)(2,1)S(1)}, u32[]{:S(2)}, u32[]{:S(2)}) collective-permute-start(bf16[2,128,1024]{2,1,0:T(8,128)(2,1)S(1)} %get-tuple-element.18), channel_id=1, source_target_pairs={{0,2},{1,3},{8,10},{9,11},{16,18},{17,19},{24,26},{25,27}} | collective-permute-start | bytes 1572872 | tf_op jit(solution)/shard_map/ppermute | solution.py:55
  63.7 24.1 %collective-permute-start.10 = (bf16[2,128,1024]{2,1,0:T(8,128)(2,1)S(1)}, bf16[2,128,1024]{2,1,0:T(8,128)(2,1)S(1)}, u32[]{:S(2)}, u32[]{:S(2)}) collective-permute-start(bf16[2,128,1024]{2,1,0:T(8,128)(2,1)S(1)} %get-tuple-element.19), channel_id=1, source_target_pairs={{6,4},{7,5},{14,12},{15,13},{22,20},{23,21},{30,28},{31,29}} | collective-permute-start | bytes 1572872 | tf_op jit(solution)/shard_map/ppermute | solution.py:56
  64.5 43.9 %collective-permute-start.14 = (bf16[4,128,1024]{2,1,0:T(8,128)(2,1)S(1)}, bf16[4,128,1024]{2,1,0:T(8,128)(2,1)S(1)}, u32[]{:S(2)}, u32[]{:S(2)}) collective-permute-start(bf16[4,128,1024]{2,1,0:T(8,128)(2,1)S(1)} %dynamic-slice_bitcast_fusion.1), channel_id=1, source_target_pairs={{0,1},{2,3},{4,5},{6,7},{1,0},{3,2},{5,4},{7,6},{8,9},{10,11},{12,... | collective-permute-start | bytes 3145736 | tf_op jit(solution)/shard_map/ppermute | solution.py:47
  73.0 16.7 %collective-permute-start.8 = (bf16[2,128,1024]{2,1,0:T(8,128)(2,1)S(1)}, bf16[2,128,1024]{2,1,0:T(8,128)(2,1)S(1)}, u32[]{:S(2)}, u32[]{:S(2)}) collective-permute-start(bf16[2,128,1024]{2,1,0:T(8,128)(2,1)S(1)} %fusion.34), channel_id=1, source_target_pairs={{0,2},{1,3},{2,4},{3,5},{8,10},{9,11},{10,12},{11,13},{16,18},{17,... | collective-permute-start | bytes 1572872 | tf_op jit(solution)/shard_map/ppermute | solution.py:55
  77.5 50.8 %collective-permute-start.21 = (bf16[4,128,1024]{2,1,0:T(8,128)(2,1)S(1)}, bf16[4,128,1024]{2,1,0:T(8,128)(2,1)S(1)}, u32[]{:S(2)}, u32[]{:S(2)}) collective-permute-start(bf16[4,128,1024]{2,1,0:T(8,128)(2,1)S(1)} %dynamic-slice_bitcast_fusion), channel_id=1, source_target_pairs={{0,1},{2,3},{4,5},{6,7},{1,0},{3,2},{5,4},{7,6},{8,9},{10,11},{12,... | collective-permute-start | bytes 3145736 | tf_op jit(solution)/shard_map/ppermute | solution.py:47
  86.4 44.0 %collective-permute-start.1 = (bf16[128,1024]{1,0:T(8,128)(2,1)S(1)}, bf16[128,1024]{1,0:T(8,128)(2,1)S(1)}, u32[]{:S(2)}, u32[]{:S(2)}) collective-permute-start(bf16[128,1024]{1,0:T(8,128)(2,1)S(1)} %get-tuple-element.14), channel_id=1, source_target_pairs={{0,2},{1,3},{8,10},{9,11},{16,18},{17,19},{24,26},{25,27}} | collective-permute-start | bytes 786440 | tf_op jit(solution)/shard_map/ppermute | solution.py:55
  87.8 55.3 %collective-permute-start.4 = (bf16[128,1024]{1,0:T(8,128)(2,1)S(1)}, bf16[128,1024]{1,0:T(8,128)(2,1)S(1)}, u32[]{:S(2)}, u32[]{:S(2)}) collective-permute-start(bf16[128,1024]{1,0:T(8,128)(2,1)S(1)} %get-tuple-element.15), channel_id=1, source_target_pairs={{6,4},{7,5},{14,12},{15,13},{22,20},{23,21},{30,28},{31,29}} | collective-permute-start | bytes 786440 | tf_op jit(solution)/shard_map/ppermute | solution.py:56
  90.2 59.7 %collective-permute-start.11 = (bf16[2,128,1024]{2,1,0:T(8,128)(2,1)S(1)}, bf16[2,128,1024]{2,1,0:T(8,128)(2,1)S(1)}, u32[]{:S(2)}, u32[]{:S(2)}) collective-permute-start(bf16[2,128,1024]{2,1,0:T(8,128)(2,1)S(1)} %get-tuple-element.17), channel_id=1, source_target_pairs={{4,2},{5,3},{6,4},{7,5},{12,10},{13,11},{14,12},{15,13},{20,18},{2... | collective-permute-start | bytes 1572872 | tf_op jit(solution)/shard_map/ppermute | solution.py:56
  108.4 76.4 %collective-permute-start.9 = (bf16[2,128,1024]{2,1,0:T(8,128)(2,1)S(1)}, bf16[2,128,1024]{2,1,0:T(8,128)(2,1)S(1)}, u32[]{:S(2)}, u32[]{:S(2)}) collective-permute-start(bf16[2,128,1024]{2,1,0:T(8,128)(2,1)S(1)} %get-tuple-element.16), channel_id=1, source_target_pairs={{0,2},{1,3},{2,4},{3,5},{4,6},{5,7},{8,10},{9,11},{10,12},{11,13},... | collective-permute-start | bytes 1572872 | tf_op jit(solution)/shard_map/ppermute | solution.py:55
  128.3 8.4 %collective-permute-start.15 = (bf16[128,1024]{1,0:T(8,128)(2,1)S(1)}, bf16[128,1024]{1,0:T(8,128)(2,1)S(1)}, u32[]{:S(2)}, u32[]{:S(2)}) collective-permute-start(bf16[128,1024]{1,0:T(8,128)(2,1)S(1)} %get-tuple-element.22), channel_id=1, source_target_pairs={{0,2},{1,3},{8,10},{9,11},{16,18},{17,19},{24,26},{25,27}} | collective-permute-start | bytes 786440 | tf_op jit(solution)/shard_map/ppermute | solution.py:55
  130.5 11.9 %collective-permute-start.22 = (bf16[128,1024]{1,0:T(8,128)(2,1)S(1)}, bf16[128,1024]{1,0:T(8,128)(2,1)S(1)}, u32[]{:S(2)}, u32[]{:S(2)}) collective-permute-start(bf16[128,1024]{1,0:T(8,128)(2,1)S(1)} %get-tuple-element.26), channel_id=1, source_target_pairs={{0,2},{1,3},{8,10},{9,11},{16,18},{17,19},{24,26},{25,27}} | collective-permute-start | bytes 786440 | tf_op jit(solution)/shard_map/ppermute | solution.py:55
  136.7 8.6 %collective-permute-start.2 = (bf16[128,1024]{1,0:T(8,128)(2,1)S(1)}, bf16[128,1024]{1,0:T(8,128)(2,1)S(1)}, u32[]{:S(2)}, u32[]{:S(2)}) collective-permute-start(bf16[128,1024]{1,0:T(8,128)(2,1)S(1)} %fusion.58), channel_id=1, source_target_pairs={{0,2},{1,3},{2,4},{3,5},{8,10},{9,11},{10,12},{11,13},{16,18},{17,... | collective-permute-start | bytes 786440 | tf_op jit(solution)/shard_map/ppermute | solution.py:55
  142.3 9.7 %collective-permute-start.18 = (bf16[128,1024]{1,0:T(8,128)(2,1)S(1)}, bf16[128,1024]{1,0:T(8,128)(2,1)S(1)}, u32[]{:S(2)}, u32[]{:S(2)}) collective-permute-start(bf16[128,1024]{1,0:T(8,128)(2,1)S(1)} %get-tuple-element.23), channel_id=1, source_target_pairs={{6,4},{7,5},{14,12},{15,13},{22,20},{23,21},{30,28},{31,29}} | collective-permute-start | bytes 786440 | tf_op jit(solution)/shard_map/ppermute | solution.py:56
  143.1 17.9 %collective-permute-start.25 = (bf16[128,1024]{1,0:T(8,128)(2,1)S(1)}, bf16[128,1024]{1,0:T(8,128)(2,1)S(1)}, u32[]{:S(2)}, u32[]{:S(2)}) collective-permute-start(bf16[128,1024]{1,0:T(8,128)(2,1)S(1)} %get-tuple-element.27), channel_id=1, source_target_pairs={{6,4},{7,5},{14,12},{15,13},{22,20},{23,21},{30,28},{31,29}} | collective-permute-start | bytes 786440 | tf_op jit(solution)/shard_map/ppermute | solution.py:56
  145.3 11.1 %collective-permute-start.16 = (bf16[128,1024]{1,0:T(8,128)(2,1)S(1)}, bf16[128,1024]{1,0:T(8,128)(2,1)S(1)}, u32[]{:S(2)}, u32[]{:S(2)}) collective-permute-start(bf16[128,1024]{1,0:T(8,128)(2,1)S(1)} %fusion.51), channel_id=1, source_target_pairs={{0,2},{1,3},{2,4},{3,5},{8,10},{9,11},{10,12},{11,13},{16,18},{17,... | collective-permute-start | bytes 786440 | tf_op jit(solution)/shard_map/ppermute | solution.py:55
  149.9 12.4 %collective-permute-start.23 = (bf16[128,1024]{1,0:T(8,128)(2,1)S(1)}, bf16[128,1024]{1,0:T(8,128)(2,1)S(1)}, u32[]{:S(2)}, u32[]{:S(2)}) collective-permute-start(bf16[128,1024]{1,0:T(8,128)(2,1)S(1)} %fusion.45), channel_id=1, source_target_pairs={{0,2},{1,3},{2,4},{3,5},{8,10},{9,11},{10,12},{11,13},{16,18},{17,... | collective-permute-start | bytes 786440 | tf_op jit(solution)/shard_map/ppermute | solution.py:55
  152.1 11.1 %collective-permute-start.5 = (bf16[128,1024]{1,0:T(8,128)(2,1)S(1)}, bf16[128,1024]{1,0:T(8,128)(2,1)S(1)}, u32[]{:S(2)}, u32[]{:S(2)}) collective-permute-start(bf16[128,1024]{1,0:T(8,128)(2,1)S(1)} %get-tuple-element.13), channel_id=1, source_target_pairs={{4,2},{5,3},{6,4},{7,5},{12,10},{13,11},{14,12},{15,13},{20,18},{2... | collective-permute-start | bytes 786440 | tf_op jit(solution)/shard_map/ppermute | solution.py:56
  156.5 31.3 %collective-permute-start.3 = (bf16[128,1024]{1,0:T(8,128)(2,1)S(1)}, bf16[128,1024]{1,0:T(8,128)(2,1)S(1)}, u32[]{:S(2)}, u32[]{:S(2)}) collective-permute-start(bf16[128,1024]{1,0:T(8,128)(2,1)S(1)} %get-tuple-element.12), channel_id=1, source_target_pairs={{0,2},{1,3},{2,4},{3,5},{4,6},{5,7},{8,10},{9,11},{10,12},{11,13},... | collective-permute-start | bytes 786440 | tf_op jit(solution)/shard_map/ppermute | solution.py:55
  161.0 25.1 %collective-permute-start.12 = (bf16[2,128,1024]{2,1,0:T(8,128)(2,1)S(1)}, bf16[2,128,1024]{2,1,0:T(8,128)(2,1)S(1)}, u32[]{:S(2)}, u32[]{:S(2)}) collective-permute-start(bf16[2,128,1024]{2,1,0:T(8,128)(2,1)S(1)} %fusion.33), channel_id=1, source_target_pairs={{2,0},{3,1},{4,2},{5,3},{6,4},{7,5},{10,8},{11,9},{12,10},{13,11},... | collective-permute-start | bytes 1572872 | tf_op jit(solution)/shard_map/ppermute | solution.py:56
  163.2 18.8 %collective-permute-start.26 = (bf16[128,1024]{1,0:T(8,128)(2,1)S(1)}, bf16[128,1024]{1,0:T(8,128)(2,1)S(1)}, u32[]{:S(2)}, u32[]{:S(2)}) collective-permute-start(bf16[128,1024]{1,0:T(8,128)(2,1)S(1)} %get-tuple-element.25), channel_id=1, source_target_pairs={{4,2},{5,3},{6,4},{7,5},{12,10},{13,11},{14,12},{15,13},{20,18},{2... | collective-permute-start | bytes 786440 | tf_op jit(solution)/shard_map/ppermute | solution.py:56
  164.1 32.7 %collective-permute-start.17 = (bf16[128,1024]{1,0:T(8,128)(2,1)S(1)}, bf16[128,1024]{1,0:T(8,128)(2,1)S(1)}, u32[]{:S(2)}, u32[]{:S(2)}) collective-permute-start(bf16[128,1024]{1,0:T(8,128)(2,1)S(1)} %get-tuple-element.20), channel_id=1, source_target_pairs={{0,2},{1,3},{2,4},{3,5},{4,6},{5,7},{8,10},{9,11},{10,12},{11,13},... | collective-permute-start | bytes 786440 | tf_op jit(solution)/shard_map/ppermute | solution.py:55
  182.0 15.1 %collective-permute-start.24 = (bf16[128,1024]{1,0:T(8,128)(2,1)S(1)}, bf16[128,1024]{1,0:T(8,128)(2,1)S(1)}, u32[]{:S(2)}, u32[]{:S(2)}) collective-permute-start(bf16[128,1024]{1,0:T(8,128)(2,1)S(1)} %get-tuple-element.24), channel_id=1, source_target_pairs={{0,2},{1,3},{2,4},{3,5},{4,6},{5,7},{8,10},{9,11},{10,12},{11,13},... | collective-permute-start | bytes 786440 | tf_op jit(solution)/shard_map/ppermute | solution.py:55
  184.8 9.3 %collective-permute-start.6 = (bf16[128,1024]{1,0:T(8,128)(2,1)S(1)}, bf16[128,1024]{1,0:T(8,128)(2,1)S(1)}, u32[]{:S(2)}, u32[]{:S(2)}) collective-permute-start(bf16[128,1024]{1,0:T(8,128)(2,1)S(1)} %fusion.57), channel_id=1, source_target_pairs={{2,0},{3,1},{4,2},{5,3},{6,4},{7,5},{10,8},{11,9},{12,10},{13,11},... | collective-permute-start | bytes 786440 | tf_op jit(solution)/shard_map/ppermute | solution.py:56
  186.1 10.8 %collective-permute-start.20 = (bf16[128,1024]{1,0:T(8,128)(2,1)S(1)}, bf16[128,1024]{1,0:T(8,128)(2,1)S(1)}, u32[]{:S(2)}, u32[]{:S(2)}) collective-permute-start(bf16[128,1024]{1,0:T(8,128)(2,1)S(1)} %fusion.50), channel_id=1, source_target_pairs={{2,0},{3,1},{4,2},{5,3},{6,4},{7,5},{10,8},{11,9},{12,10},{13,11},... | collective-permute-start | bytes 786440 | tf_op jit(solution)/shard_map/ppermute | solution.py:56
  187.7 12.0 %collective-permute-start.27 = (bf16[128,1024]{1,0:T(8,128)(2,1)S(1)}, bf16[128,1024]{1,0:T(8,128)(2,1)S(1)}, u32[]{:S(2)}, u32[]{:S(2)}) collective-permute-start(bf16[128,1024]{1,0:T(8,128)(2,1)S(1)} %fusion.44), channel_id=1, source_target_pairs={{2,0},{3,1},{4,2},{5,3},{6,4},{7,5},{10,8},{11,9},{12,10},{13,11},... | collective-permute-start | bytes 786440 | tf_op jit(solution)/shard_map/ppermute | solution.py:56
  223.6 69.0 %collective-permute-start.30 = (bf16[1024,512]{1,0:T(8,128)(2,1)}, bf16[1024,512]{1,0:T(8,128)(2,1)}, u32[]{:S(2)}, u32[]{:S(2)}) collective-permute-start(bf16[1024,512]{1,0:T(8,128)(2,1)} %broadcast_select_fusion), channel_id=1, source_target_pairs={{8,0},{24,16},{9,1},{25,17},{10,2},{26,18},{11,3},{27,19},{12,4},{... | collective-permute-start | bytes 3145736 | tf_op jit(solution)/shard_map/ppermute | solution.py:126
  227.0 65.6 %collective-permute-start.28 = (bf16[128,4096]{1,0:T(8,128)(2,1)S(1)}, bf16[128,4096]{1,0:T(8,128)(2,1)S(1)}, u32[]{:S(2)}, u32[]{:S(2)}) collective-permute-start(bf16[128,4096]{1,0:T(8,128)(2,1)S(1)} %get-tuple-element.9), channel_id=1, source_target_pairs={{0,8},{8,16},{16,24},{1,9},{9,17},{17,25},{2,10},{10,18},{18,26},{... | collective-permute-start | bytes 3145736 | tf_op jit(solution)/shard_map/ppermute | solution.py:122
  (21 other events, 171.5 us)
Sparse Core Ops, SparseCore 0:
  34.1 18.0 all-gather.3
  220.9 50.8 all-gather.5

commit v2 on v1

--- a/solution.py
+++ b/solution.py
@@ -1,12 +1,20 @@
+import functools
+
 import jax
 import jax.numpy as jnp
 from jax import lax
+from jax.experimental import pallas as pl
+from jax.experimental.pallas import tpu as pltpu
 from jax.sharding import PartitionSpec as P
 
 EPS = 1e-05
 ALPHA = 1.5
 BF = jnp.bfloat16
 F32 = jnp.float32
+MESH = pl.DeviceIdType.MESH
+CHUNKS = 8
+HALVES = 2
+VMEM_MAX = 48 << 20
 
 
 def rms_scale(values):
@@ -60,6 +68,470 @@
 def spread_pairs(size, bit):
     low = (1 << (bit + 1)) - 1
     return [(i, i ^ (1 << bit)) for i in range(size) if i & low == low]
+
+
+def remote(src, dst, send, recv, **place):
+    return pltpu.make_async_remote_copy(
+        src_ref=src, dst_ref=dst, send_sem=send, recv_sem=recv, device_id=place,
+        device_id_type=MESH,
+    )
+
+
+def greet(fsdp, sections):
+    me, section = lax.axis_index("fsdp"), lax.axis_index("section")
+    barrier = pltpu.get_barrier_semaphore()
+    for j in range(1, fsdp):
+        pl.semaphore_signal(
+            barrier, inc=1, device_id={"fsdp": lax.rem(me + j, fsdp)}, device_id_type=MESH
+        )
+    for j in range(1, sections):
+        pl.semaphore_signal(
+            barrier, inc=1, device_id={"section": lax.rem(section + j, sections)},
+            device_id_type=MESH,
+        )
+    pl.semaphore_wait(barrier, fsdp + sections - 2)
+
+
+def project_kernel(
+    fsdp, sections, planes, chunks,
+    hidden, gain, weight, pre, feat,
+    normed, tokens, part, y_in, z_in, z_in0,
+    tok_send, tok_recv, y_send, y_recv, z_send, z_recv, f_send, f_recv,
+):
+    me, section = lax.axis_index("fsdp"), lax.axis_index("section")
+    y, z = lax.rem(me, 2), me // 2
+    rows, features = hidden.shape
+    depth = features // fsdp
+    width = features // chunks
+    last = sections - 1
+    greet(fsdp, sections)
+
+    @pl.loop(0, rows // 16)
+    def _(i):
+        r = pl.ds(pl.multiple_of(i * 16, 16), 16)
+        normed[r, :] = (rms_scale(hidden[r, :].astype(F32)) * gain[...]).astype(BF)
+
+    def token_copy(j):
+        to = lax.rem(me + j, fsdp)
+        return remote(
+            normed.at[:, pl.ds(pl.multiple_of(to * depth, 128), depth)], tokens.at[y, z],
+            tok_send.at[j - 1], tok_recv.at[j - 1], fsdp=to,
+        )
+
+    for j in range(1, fsdp):
+        token_copy(j).start()
+    tokens[y, z] = normed[:, pl.ds(pl.multiple_of(me * depth, 128), depth)]
+    for j in range(1, fsdp):
+        token_copy(j).wait_recv()
+
+    def feature_copy(to):
+        return remote(tokens, feat, f_send.at[to], f_recv, section=to)
+
+    @pl.when(section == last)
+    def _():
+        for to in range(last):
+            feature_copy(to).start()
+        feat[...] = tokens[...]
+
+    def y_copy(c):
+        return remote(
+            part.at[c, 1 - y], y_in.at[c], y_send.at[c], y_recv.at[c], fsdp=z * 2 + 1 - y
+        )
+
+    def y_copy0():
+        return remote(
+            part.at[0, 1 - y, z], y_in.at[0, 0], y_send.at[0], y_recv.at[0], fsdp=z * 2 + 1 - y
+        )
+
+    def z_copy(c, way, t):
+        d = planes - t + z if way == 0 else z - planes + t
+        d = jnp.minimum(jnp.maximum(d, 0), planes - 1)
+        to = jnp.minimum(z + 1, planes - 1) if way == 0 else jnp.maximum(z - 1, 0)
+        if isinstance(c, int):
+            src, dst = part.at[0, :, d], z_in0.at[way, t - 1]
+        else:
+            src, dst = part.at[c, y, d], z_in.at[c, way, t - 1]
+        return d, remote(
+            src, dst, z_send.at[c, way, t - 1], z_recv.at[c, way, t - 1], fsdp=to * 2 + y
+        )
+
+    def sends(way, t):
+        if way == 0:
+            return (z <= t - 1) & (z < planes - 1)
+        return (z >= planes - t) & (z > 0)
+
+    def receives(way, t):
+        if way == 0:
+            return (z >= 1) & (z <= t)
+        return (z <= planes - 2) & (z >= planes - 1 - t)
+
+    def z_start(c, t):
+        for way in range(2):
+            d, copy = z_copy(c, way, t)
+            if t > 1:
+
+                @pl.when(sends(way, t) & receives(way, t - 1))
+                def _():
+                    z_copy(c, way, t - 1)[1].wait_recv()
+                    if isinstance(c, int):
+                        for k in range(2):
+                            part[0, k, d] = (
+                                part[0, k, d].astype(F32) + z_in0[way, t - 2, k].astype(F32)
+                            ).astype(BF)
+                    else:
+                        part[c, y, d] = (
+                            part[c, y, d].astype(F32) + z_in[c, way, t - 2].astype(F32)
+                        ).astype(BF)
+
+            @pl.when(sends(way, t))
+            def _():
+                copy.start()
+
+    def z_last(c):
+        t = planes - 1
+        for way in range(2):
+
+            @pl.when(receives(way, t))
+            def _():
+                z_copy(c, way, t)[1].wait_recv()
+                if isinstance(c, int):
+                    for k in range(2):
+                        part[0, k, z] = (
+                            part[0, k, z].astype(F32) + z_in0[way, t - 1, k].astype(F32)
+                        ).astype(BF)
+                else:
+                    part[c, y, z] = (
+                        part[c, y, z].astype(F32) + z_in[c, way, t - 1].astype(F32)
+                    ).astype(BF)
+
+    ahead = min(3, chunks - 1)
+
+    @pl.loop(0, chunks)
+    def _(c):
+        block = weight[:, pl.ds(pl.multiple_of(c * width, 128), width)]
+        for k in range(2):
+            part[c, k] = (
+                jnp.dot(
+                    tokens[k].reshape(planes * rows, depth), block, preferred_element_type=F32
+                )
+                .astype(BF)
+                .reshape(planes, rows, width)
+            )
+
+        @pl.when(c == 0)
+        def _():
+            z_start(0, 1)
+
+        @pl.when((c >= 1) & (c <= ahead))
+        def _():
+            y_copy(c).start()
+
+    @pl.loop(1, chunks + planes - 1)
+    def _(i):
+        for t in range(1, planes):
+
+            @pl.when(i == t)
+            def _():
+                if t < planes - 1:
+                    z_start(0, t + 1)
+                else:
+                    z_last(0)
+                    y_copy0().start()
+
+        @pl.when(i < chunks)
+        def _():
+            y_copy(i).wait_recv()
+
+            @pl.when(i + ahead < chunks)
+            def _():
+                y_copy(i + ahead).start()
+
+            for d in range(planes):
+                part[i, y, d] = (part[i, y, d].astype(F32) + y_in[i, d].astype(F32)).astype(BF)
+            z_start(i, 1)
+
+        for t in range(1, planes - 1):
+            c = i - t
+
+            @pl.when((c >= 1) & (c < chunks))
+            def _():
+                z_start(c, t + 1)
+
+        c = i - (planes - 1)
+
+        @pl.when((c >= 1) & (c < chunks))
+        def _():
+            z_last(c)
+            pre[:, pl.ds(pl.multiple_of(c * width, 128), width)] = part[c, y, z]
+
+    y_copy0().wait_recv()
+    pre[:, pl.ds(0, width)] = (part[0, y, z].astype(F32) + y_in[0, 0].astype(F32)).astype(BF)
+
+    @pl.when(section != last)
+    def _():
+        feature_copy(0).wait_recv()
+
+    @pl.when(section == last)
+    def _():
+        for to in range(last):
+            feature_copy(to).wait_send()
+
+    for j in range(1, fsdp):
+        token_copy(j).wait_send()
+    y_copy0().wait_send()
+    for t in range(1, planes):
+        for way in range(2):
+
+            @pl.when(sends(way, t))
+            def _():
+                z_copy(0, way, t)[1].wait_send()
+
+    @pl.loop(1, chunks)
+    def _(c):
+        y_copy(c).wait_send()
+        for t in range(1, planes):
+            for way in range(2):
+
+                @pl.when(sends(way, t))
+                def _():
+                    z_copy(c, way, t)[1].wait_send()
+
+
+def project(hidden, gain, weight, fsdp, sections):
+    rows, features = hidden.shape
+    planes, chunks = fsdp // 2, CHUNKS
+    depth, width = features // fsdp, features // chunks
+    dma = pltpu.SemaphoreType.DMA
+    vmem = pl.BlockSpec(memory_space=pltpu.VMEM)
+    return pl.pallas_call(
+        functools.partial(project_kernel, fsdp, sections, planes, chunks),
+        out_shape=(
+            jax.ShapeDtypeStruct((rows, features), BF),
+            jax.ShapeDtypeStruct((2, planes, rows, depth), BF),
+        ),
+        in_specs=[vmem] * 3,
+        out_specs=(vmem, vmem),
+        scratch_shapes=[
+            pltpu.VMEM((rows, features), BF),
+            pltpu.VMEM((2, planes, rows, depth), BF),
+            pltpu.VMEM((chunks, 2, planes, rows, width), BF),
+            pltpu.VMEM((chunks, planes, rows, width), BF),
+            pltpu.VMEM((chunks, 2, planes - 1, rows, width), BF),
+            pltpu.VMEM((2, planes - 1, 2, rows, width), BF),
+            dma((fsdp - 1,)),
+            dma((fsdp - 1,)),
+            dma((chunks,)),
+            dma((chunks,)),
+            dma((chunks, 2, planes - 1)),
+            dma((chunks, 2, planes - 1)),
+            dma((sections,)),
+            dma,
+        ],
+        compiler_params=pltpu.CompilerParams(
+            collective_id=0, has_side_effects=True, vmem_limit_bytes=VMEM_MAX
+        ),
+        cost_estimate=pl.CostEstimate(
+            flops=2 * fsdp * rows * depth * features, bytes_accessed=1 << 23, transcendentals=0
+        ),
+    )(hidden, gain, weight)
+
+
+def gather_kernel(
+    fsdp, sections, planes,
+    cot, stats, cols, table,
+    x_send, x_recv, sx_send, sx_recv, st_send, st_recv, z_send, z_recv, y_send, y_recv,
+):
+    me, section = lax.axis_index("fsdp"), lax.axis_index("section")
+    y, z = lax.rem(me, 2), me // 2
+    last = sections - 1
+    rows, features = cot.shape
+    width = features // sections
+    size = rows // HALVES
+    greet(fsdp, sections)
+
+    def stats_x(to):
+        return remote(stats, table.at[y, z], sx_send.at[to], sx_recv, section=to)
+
+    def cols_x(to, h):
+        return remote(
+            cot.at[pl.ds(h * size, size), pl.ds(to * width, width)], cols.at[y, z, h],
+            x_send.at[to, h], x_recv.at[h], section=to,
+        )
+
+    def stats_f(j):
+        return remote(
+            table.at[y, z], table.at[y, z], st_send.at[j - 1], st_recv.at[j - 1],
+            fsdp=lax.rem(me + j, fsdp),
+        )
+
+    def y_copy(plane, h):
+        block = cols.at[y, plane, h]
+        return remote(
+            block, block, y_send.at[plane, h], y_recv.at[plane, h], fsdp=z * 2 + 1 - y
+        )
+
+    def z_copy(way, t, h):
+        if way == 0:
+            plane, to = jnp.maximum(z - t + 1, 0), jnp.minimum(z + 1, planes - 1)
+        else:
+            plane, to = jnp.minimum(z + t - 1, planes - 1), jnp.maximum(z - 1, 0)
+        block = cols.at[y, plane, h]
+        return remote(
+            block, block, z_send.at[way, t - 1, h], z_recv.at[way, t - 1, h], fsdp=to * 2 + y
+        )
+
+    def sends(way, t):
+        if way == 0:
+            return (z < planes - 1) & (z - t + 1 >= 0)
+        return (z > 0) & (z + t - 1 <= planes - 1)
+
+    def receives(way, t):
+        return z - t >= 0 if way == 0 else z + t <= planes - 1
+
+    @pl.when(section == last)
+    def _():
+        for to in range(last):
+            stats_x(to).start()
+        for h in range(HALVES):
+            for to in range(last):
+                cols_x(to, h).start()
+        table[y, z] = stats[...]
+        for h in range(HALVES):
+            cols[y, z, h] = cot[pl.ds(h * size, size), pl.ds(last * width, width)]
+
+    @pl.when(section != last)
+    def _():
+        stats_x(0).wait_recv()
+
+    for j in range(1, fsdp):
+        stats_f(j).start()
+    for h in range(HALVES):
+
+        @pl.when(section != last)
+        def _():
+            cols_x(0, h).wait_recv()
+
+        for way in range(2):
+
+            @pl.when(sends(way, 1))
+            def _():
+                z_copy(way, 1, h).start()
+
+        y_copy(z, h).start()
+    for t in range(1, planes):
+        for h in range(HALVES):
+            for way in range(2):
+
+                @pl.when(receives(way, t))
+                def _():
+                    z_copy(way, t, h).wait_recv()
+                    y_copy(z - t if way == 0 else z + t, h).start()
+
+                if t < planes - 1:
+
+                    @pl.when(sends(way, t + 1))
+                    def _():
+                        z_copy(way, t + 1, h).start()
+
+    for j in range(1, fsdp):
+        stats_f(j).wait()
+    for plane in range(planes):
+        for h in range(HALVES):
+            y_copy(plane, h).wait()
+    for t in range(1, planes):
+        for h in range(HALVES):
+            for way in range(2):
+
+                @pl.when(sends(way, t))
+                def _():
+                    z_copy(way, t, h).wait_send()
+
+    @pl.when(section == last)
+    def _():
+        for to in range(last):
+            stats_x(to).wait_send()
+            for h in range(HALVES):
+                cols_x(to, h).wait_send()
+
+
+def gather(cot, stats, fsdp, sections):
+    rows, features = cot.shape
+    planes = fsdp // 2
+    width = features // sections
+    dma = pltpu.SemaphoreType.DMA
+    vmem = pl.BlockSpec(memory_space=pltpu.VMEM)
+    return pl.pallas_call(
+        functools.partial(gather_kernel, fsdp, sections, planes),
+        out_shape=(
+            jax.ShapeDtypeStruct((2, planes, HALVES, rows // HALVES, width), BF),
+            jax.ShapeDtypeStruct((2, planes) + stats.shape, F32),
+        ),
+        in_specs=[vmem] * 2,
+        out_specs=(vmem, vmem),
+        scratch_shapes=[
+            dma((sections, HALVES)),
+            dma((HALVES,)),
+            dma((sections,)),
+            dma,
+            dma((fsdp - 1,)),
+            dma((fsdp - 1,)),
+            dma((2, planes - 1, HALVES)),
+            dma((2, planes - 1, HALVES)),
+            dma((planes, HALVES)),
+            dma((planes, HALVES)),
+        ],
+        compiler_params=pltpu.CompilerParams(
+            collective_id=1, has_side_effects=True, vmem_limit_bytes=VMEM_MAX
+        ),
+        cost_estimate=pl.CostEstimate(flops=0, bytes_accessed=1 << 23, transcendentals=0),
+    )(cot, stats)
+
+
+def kernels_fit(rows, features, fsdp, sections):
+    if fsdp < 4 or fsdp % 2 or sections < 2:
+        return False
+    planes = fsdp // 2
+    block = rows * features * 2
+    planned = block * (2 * planes + planes + 2 * planes - 2 + 7) + features // fsdp * features * 2
+    return (
+        planned <= VMEM_MAX * 3 // 4
+        and rows % (16 * HALVES) == 0
+        and CHUNKS >= planes + 1
+        and features % (128 * CHUNKS) == 0
+        and features % (128 * fsdp) == 0
+        and features % (128 * sections) == 0
+        and 1 << ((fsdp.bit_length() - 1) // 2) == 2
+    )
+
+
+def project_permuted(feature_block, weight, rows, y_size, z_size, y_place, z_place):
+    features = weight.shape[1]
+    chunks = 4
+    width = features // chunks
+    pieces = []
+    for c in range(chunks):
+        partial = jnp.dot(
+            feature_block, weight[:, c * width : (c + 1) * width], preferred_element_type=F32
+        ).astype(BF)
+        partial = partial.reshape(z_size, y_size, rows, width)
+        if c == 1:
+            partial = line_reduce_scatter(partial, z_place, z_size, y_size, y_size)
+            total = line_reduce_scatter(partial, y_place, y_size, 1, 1)
+        else:
+            partial = line_reduce_scatter(partial.swapaxes(0, 1), y_place, y_size, 1, 1)
+            total = line_reduce_scatter(partial, z_place, z_size, y_size, y_size)
+        pieces.append(total.astype(BF))
+    return jnp.concatenate(pieces, axis=1)
+
+
+def from_last(feature_all, section_index, section_size):
+    for bit in reversed(range(section_size.bit_length() - 1)):
+        got = lax.ppermute(feature_all, "section", spread_pairs(section_size, bit))
+        takes = (section_index >> bit & 1 == 0) & (
+            section_index & ((1 << bit) - 1) == (1 << bit) - 1
+        )
+        feature_all = jnp.where(takes, got, feature_all)
+    return feature_all
 
 
 def local(
@@ -88,9 +560,16 @@
 
     hidden = activations[0]
     rows, features = hidden.shape
-    normed = (rms_scale(hidden.astype(F32)) * norm_gain[0]).astype(BF)
-    feature_block = lax.all_to_all(normed, "fsdp", split_axis=1, concat_axis=0, tiled=True)
     weight = trunk_weight[0]
+    fused = kernels_fit(rows, features, fsdp_size, section_size)
+    if fused:
+        pre, feature_all = project(hidden, norm_gain, weight, fsdp_size, section_size)
+        feature_all = feature_all.reshape(fsdp_size * rows, features // fsdp_size)
+    else:
+        normed = (rms_scale(hidden.astype(F32)) * norm_gain[0]).astype(BF)
+        feature_block = lax.all_to_all(normed, "fsdp", split_axis=1, concat_axis=0, tiled=True)
+        pre = project_permuted(feature_block, weight, rows, y_size, z_size, y_place, z_place)
+        feature_all = from_last(feature_block, section_index, section_size)
 
     wanted = head_weight[task_of[:, 0]]
     if head_rows % section_size == 0 and (head_rows // section_size) % 16 == 0:
@@ -102,32 +581,8 @@
         part = lax.all_to_all(wanted, "fsdp", split_axis=0, concat_axis=0, tiled=True)
     head_w = part.reshape(features, outs)
 
-    chunks = 4
-    width = features // chunks
-    pieces = []
-    for c in range(chunks):
-        partial = jnp.dot(
-            feature_block, weight[:, c * width : (c + 1) * width], preferred_element_type=F32
-        ).astype(BF)
-        partial = partial.reshape(z_size, y_size, rows, width)
-        if c == 1:
-            partial = line_reduce_scatter(partial, z_place, z_size, y_size, y_size)
-            total = line_reduce_scatter(partial, y_place, y_size, 1, 1)
-        else:
-            partial = line_reduce_scatter(partial.swapaxes(0, 1), y_place, y_size, 1, 1)
-            total = line_reduce_scatter(partial, z_place, z_size, y_size, y_size)
-        pieces.append(total.astype(BF))
-    pre = jnp.concatenate(pieces, axis=1)
     output = (hidden.astype(F32) + jax.nn.silu(pre.astype(F32))).astype(BF)
     passed = lax.ppermute(output, "section", [(i, i + 1) for i in range(section_size - 1)])
-
-    feature_all = feature_block
-    for bit in reversed(range(section_bits)):
-        got = lax.ppermute(feature_all, "section", spread_pairs(section_size, bit))
-        takes = (section_index >> bit & 1 == 0) & (
-            section_index & ((1 << bit) - 1) == (1 << bit) - 1
-        )
-        feature_all = jnp.where(takes, got, feature_all)
 
     task_id = task_of[member, 0]
     onehot = (task_of[:, 0][:, None] == jnp.arange(tasks)[None, :]).astype(F32)
@@ -147,23 +602,30 @@
     cotangent = (grad_out * slope_term).astype(BF)
 
     col_width = features // section_size
-    cols = cotangent.reshape(rows, section_size, col_width)
-    for bit in reversed(range(section_bits)):
-        half = cols.reshape(rows, 2, cols.shape[1] // 2, col_width)
-        low, high = half[:, 0], half[:, 1]
-        got = lax.ppermute(low, "section", spread_pairs(section_size, bit))
-        cols = jnp.where(section_index >> bit & 1 == 0, got, high)
-    column_block = lax.all_gather(cols[:, 0], "fsdp", axis=0, tiled=True)
-
     sums = jnp.concatenate([own_task * square, own_task * block_loss])
-    sums = lax.psum(jnp.where(is_last, sums, jnp.zeros_like(sums)), ("section", "fsdp"))
+    if fused:
+        stats = jnp.broadcast_to(jnp.pad(sums, (0, 128 - 2 * tasks))[None, :], (8, 128))
+        column_block, table = gather(cotangent, stats, fsdp_size, section_size)
+        sums = jnp.sum(table[:, :, 0, : 2 * tasks], axis=(0, 1))
+        column_block = column_block.reshape(fsdp_size * rows, col_width)
+        order = onehot.reshape(z_size, y_size, tasks).swapaxes(0, 1).reshape(fsdp_size, tasks)
+    else:
+        cols = cotangent.reshape(rows, section_size, col_width)
+        for bit in reversed(range(section_bits)):
+            half = cols.reshape(rows, 2, cols.shape[1] // 2, col_width)
+            low, high = half[:, 0], half[:, 1]
+            got = lax.ppermute(low, "section", spread_pairs(section_size, bit))
+            cols = jnp.where(section_index >> bit & 1 == 0, got, high)
+        column_block = lax.all_gather(cols[:, 0], "fsdp", axis=0, tiled=True)
+        sums = lax.psum(jnp.where(is_last, sums, jnp.zeros_like(sums)), ("section", "fsdp"))
+        order = onehot
     norm_sums, loss_sums = sums[:tasks], sums[tasks:]
     grad_norms = jnp.sqrt(norm_sums)
     ratios = jnp.mean(grad_norms) * loss_ratio**ALPHA / grad_norms
     task_weights = tasks * ratios / jnp.sum(ratios)
     task_losses = loss_sums / (counts * outs)
 
-    block_weight = jnp.sum(onehot * task_weights[None, :], axis=1)
+    block_weight = jnp.sum(order * task_weights[None, :], axis=1)
     scaled = (
         column_block.reshape(fsdp_size, rows, col_width).astype(F32)
         * block_weight[:, None, None]

time: 306 us -> 235 us (0.77)
  Pallas kernels: 0 us -> 170 us
  waiting for transfers between devices: 96.9 us -> 0.04 us
  starting transfers between devices: 97.7 us -> 1.51 us
  blocking collectives: 44 us -> 16.1 us
  matrix products: 16.7 us -> 9.32 us
  other arithmetic: 19.8 us -> 12.9 us
  local copies, waits for them, and re-layouts: 11.1 us -> 5.97 us
    pallas_call x0 -> x2, Pallas kernels: none -> 170 us  [the longest x1 129 us: project(): pl.pallas_call(functools.partial(project_kernel, fsdp, sections, planes,...]
    ppermute x32 -> x0, waiting for transfers between devices: 73.5 us -> none  [the longest x4 44.9 us: line_reduce_scatter(): lax.ppermute(pick(1 - place).astype(BF), 'fsdp', swap).astype(F32)]
    ppermute x32 -> x0, starting transfers between devices: 67.9 us -> none  [the longest x12 47 us: line_reduce_scatter(): lax.ppermute(send_right.astype(BF), 'fsdp', pairs(1, lambda s: s <= t - 1))]
    psum x1 -> x0, blocking collectives: 44 us -> none  [local(): lax.psum(jnp.where(is_last, sums, jnp.zeros_like(sums)), ('section', 'fsd...]
    all_to_all x2 -> x0, waiting for transfers between devices: 23.3 us -> none  [the longest x1 21.4 us: local(): lax.all_to_all(normed, 'fsdp', split_axis=1, concat_axis=0, tiled=True)]
    ppermute x1, starting transfers between devices: 18.2 us -> 1.48 us  [local(): lax.ppermute(output, 'section', [(i, i + 1) for i in range(section_size -...]
    all_to_all x0 -> x1, blocking collectives: none -> 16.1 us  [local(): part = lax.all_to_all(part, 'fsdp', split_axis=0, concat_axis=0, tiled=True)]
    all_to_all x2 -> x0, starting transfers between devices: 11.4 us -> none  [the longest x1 7.28 us: local(): part = lax.all_to_all(part, 'fsdp', split_axis=0, concat_axis=0, tiled=True)]
  transfers between devices with their start and end apart: 37 -> 2, of which waited for: 15 -> 0; matrix products, arithmetic and copies ran while one was open for 8% -> 1% of each run, Pallas kernels for 0% -> 55%
where the time goes in v2:
time: 235 us; the launch traced here: 234 us
  Pallas kernels  170 us (72%)
  between operations  18.2 us (8%)
  blocking collectives  16.1 us (7%)
  other arithmetic  12.9 us (5%)
  matrix products  9.32 us (4%)
  local copies, waits for them, and re-layouts  5.97 us (3%)
    pallas_call x1, Pallas kernels, project(): pl.pallas_call(functools.partial(project_kernel, fsdp, sections, planes,...  129 us
    pallas_call x1, Pallas kernels, gather(): pl.pallas_call(functools.partial(gather_kernel, fsdp, sections, planes),...  40.9 us
    all_to_all x1, blocking collectives, local(): part = lax.all_to_all(part, 'fsdp', split_axis=0, concat_axis=0, tiled=True)  16.1 us
  transfers between devices with their start and end apart: 2, of which 0 were waited for; matrix products, arithmetic and copies ran while one was open for 1% of the time, Pallas kernels for 55%

profile of v2, /device:TPU:0, one launch (start us, length us, event | category | flops | bytes accessed | tf_op | source)
XLA Modules:
  0.0 234.2 jit_solution(1492141049796273313)
XLA Ops:
  7.3 0.5 broadcast.132
  7.8 1.3 fusion.80
  9.1 0.7 gather_fusion
  9.9 16.1 %all_to_all.5 = bf16[8,128,128]{2,1,0:T(8,128)(2,1)} all-to-all(bf16[8,128,128]{2,1,0:T(8,128)(2,1)S(1)} %constant_dynamic-slice_fusion.1), channel_id=1, replica_groups=mesh['section'=4,'fsdp'=8] {'fsdp'}, dimensions={0} | all-to-all | bytes 524288 | tf_op jit(solution)/shard_map/all_to_all | solution.py:578
  26.0 129.3 %shard_map.120 = (bf16[128,4096]{1,0:T(8,128)(2,1)S(1)}, bf16[2,4,128,512]{3,2,1,0:T(8,128)(2,1)S(1)}) custom-call(bf16[128,4096]{1,0:T(8,128)(2,1)S(1)} %bitcast.51, f32[1,4096]{1,0:T(1,128)S(1)} %copy-done.5, bf16[512,4096]{1,0:T(8,128)(2,1)} %bitcast.58), custom_call_target="tpu_custom_call" | custom-call | flops 4294967296 | bytes 8388608 | tf_op jit(solution)/shard_map/pallas_call | solution.py:306
  155.3 1.0 copy-done.2
  156.3 1.8 fusion.10
  158.1 1.5 collective-permute-start
  159.6 0.6 constant_dynamic-slice_fusion
  162.2 0.6 dynamic_slice.14
  163.6 0.1 convert_reduce_fusion
  163.8 2.4 %fusion.13 = f32[128,128]{1,0:T(8,128)S(1)} fusion(bf16[4096,128]{1,0:T(8,128)(2,1)} %bitcast.53, bf16[128,4096]{1,0:T(8,128)(2,1)} %get-tuple-element.15, f32[128]{0:T(128)S(1)} %fusion.72), kind=kOutput, calls=%fused_computation.33 | convolution fusion | flops 135790592 | bytes 2163200 | tf_op jit(solution)/shard_map/jvp()/dot_general | solution.py:26
  166.2 0.2 convolution_tanh_fusion.3
  166.4 0.2 multiply_add_fusion.1
  166.6 0.2 multiply_add_fusion
  166.9 0.8 multiply_reduce_fusion.1
  167.7 0.3 convolution_add_fusion.3
  168.0 0.3 convolution_add_fusion.2
  168.3 0.3 convolution_add_fusion.1
  168.5 0.3 convolution_add_fusion
  168.8 1.7 fusion.12
  170.6 3.2 %multiply_reduce_fusion = (f32[]{:T(128)}, bf16[128,4096]{1,0:T(8,128)(2,1)S(1)}) fusion(bf16[128,4096]{1,0:T(8,128)(2,1)} %get-tuple-element.15, f32[128,4096]{1,0:T(8,128)S(1)} %get-tuple-element.26, f32[128]{0:T(128)S(1)} %multiply_multiply_fusion, f32[128]{0:T(128)S(1)} %fusion.72, bf16[128,4096]{1,0:T(8,128)(2,1)S(1)} %get-tuple-element.8), kind=kLoop, calls=%fused_computation.24 | loop fusion | flops 8912895 | bytes 5243908 | tf_op jit(solution)/shard_map/reduce_sum | solution.py:598
  174.4 1.3 compare_select_fusion.3
  175.8 40.9 %shard_map.121 = (bf16[2,4,2,64,1024]{4,3,2,1,0:T(8,128)(2,1)S(1)}, f32[2,4,8,128]{3,2,1,0:T(8,128)S(1)}) custom-call(bf16[128,4096]{1,0:T(8,128)(2,1)S(1)} %get-tuple-element.17.cot, f32[8,128]{1,0:T(8,128)S(1)} %broadcast_in_dim.11.stats), custom_call_target="tpu_custom_call" | custom-call | bytes 8388608 | tf_op jit(solution)/shard_map/pallas_call | solution.py:463
  216.7 1.3 copy-done.1
  218.0 0.6 fusion.73
  219.3 1.2 fusion.78
  220.5 0.6 multiply_divide_fusion.1
  221.2 0.2 select_reduce_fusion
  221.3 2.5 %multiply_convert_fusion = bf16[2,4,2,64,1024]{4,3,2,1,0:T(8,128)(2,1)S(1)} fusion(bf16[2,4,2,64,1024]{4,3,2,1,0:T(8,128)(2,1)} %copy-done.1, f32[2,4]{1,0:T(2,128)S(1)} %select_reduce_fusion), kind=kLoop, calls=%fused_computation.3 | loop fusion | flops 3145728 | bytes 4194336 | tf_op jit(solution)/shard_map/convert_element_type | solution.py:632
  223.8 2.6 %fusion.81 = f32[512,1024]{1,0:T(8,128)} fusion(bf16[1024,512]{1,0:T(8,128)(2,1)S(1)} %bitcast.50, bf16[1024,1024]{1,0:T(8,128)(2,1)S(1)} %bitcast.52), kind=kOutput, calls=%fused_computation.123 | convolution fusion | flops 1073741824 | bytes 5242880 | tf_op jit(solution)/shard_map/dot_general | solution.py:633
  226.4 1.0 copy.17
  (41 shorter events, 0.5 us)
Async XLA Ops:
  7.2 1.9 copy-start
  7.2 18.8 %copy-start.4 = (bf16[1,128,4096]{2,1,0:T(8,128)(2,1)S(1)}, bf16[1,128,4096]{2,1,0:T(8,128)(2,1)}, u32[]{:S(2)}) copy-start(bf16[1,128,4096]{2,1,0:T(8,128)(2,1)} %param.9) | copy-start | bytes 3145732
  7.2 18.8 %copy-start.5 = (f32[1,4096]{1,0:T(1,128)S(1)}, f32[1,4096]{1,0:T(1,128)}, u32[]{:S(2)}) copy-start(f32[1,4096]{1,0:T(1,128)} %gain.1) | copy-start | bytes 49156
  7.2 156.6 %all-gather.2.cloned.1.call-start = ((), (), s32[]{:S(2)}) async-start(), calls=%async_computation.1 | async-start | bytes 1310720 | tf_op jit(solution)/shard_map/all_gather | solution.py:579
  155.3 1.0 copy-start.2
  156.3 3.3 %copy-start.12 = (s32[8,1]{0,1:T(1,128)S(1)}, s32[8,1]{0,1:T(1,128)}, u32[]{:S(2)}) copy-start(s32[8,1]{0,1:T(1,128)} %param.15) | copy-start | bytes 100
  156.3 5.8 %copy-start.14 = (s32[4]{0:T(128)S(1)}, s32[4]{0:T(128)}, u32[]{:S(2)}) copy-start(s32[4]{0:T(128)} %param.14) | copy-start | bytes 52
  156.3 9.9 %copy-start.9 = (f32[4,128,128]{2,1,0:T(8,128)S(1)}, f32[4,128,128]{2,1,0:T(8,128)}, u32[]{:S(2)}) copy-start(f32[4,128,128]{2,1,0:T(8,128)} %param.13) | copy-start | bytes 786436
  158.1 8.7 %copy-start.10 = (bf16[128,128]{1,0:T(8,128)(2,1)S(1)}, bf16[128,128]{1,0:T(8,128)(2,1)}, u32[]{:S(2)}) copy-start(bf16[128,128]{1,0:T(8,128)(2,1)} %param.17) | copy-start | bytes 98308
  158.1 5.6 %collective-permute-start = (bf16[128,4096]{1,0:T(8,128)(2,1)}, bf16[128,4096]{1,0:T(8,128)(2,1)S(1)}, u32[]{:S(2)}, u32[]{:S(2)}) collective-permute-start(bf16[128,4096]{1,0:T(8,128)(2,1)} %get-tuple-element.15), channel_id=1, source_target_pairs={{0,8},{8,16},{16,24},{1,9},{9,17},{17,25},{2,10},{10,18},{18,26},{... | collective-permute-start | bytes 3145736 | tf_op jit(solution)/shard_map/ppermute | solution.py:585
  163.7 5.1 %copy-start.7 = (bf16[128,4096]{1,0:T(8,128)(2,1)}, bf16[128,4096]{1,0:T(8,128)(2,1)S(1)}, u32[]{:S(2)}) copy-start(bf16[128,4096]{1,0:T(8,128)(2,1)S(1)} %collective-permute-done) | copy-start | bytes 3145732
  163.8 5.1 %copy-start.6 = (bf16[8,512,128]{2,1,0:T(8,128)(2,1)S(1)}, bf16[8,512,128]{2,1,0:T(8,128)(2,1)}, u32[]{:S(2)}) copy-start(bf16[8,512,128]{2,1,0:T(8,128)(2,1)} %all-gather.2.cloned.1.call-done) | copy-start | bytes 3145732
  170.6 48.7 %copy-start.13 = (f32[4]{0:T(128)S(1)}, f32[4]{0:T(128)}, u32[]{:S(2)}) copy-start(f32[4]{0:T(128)} %param.16) | copy-start | bytes 52
  216.7 1.3 copy-start.1
  221.2 2.7 %copy-start.11 = (f32[4]{0:T(128)}, f32[4]{0:T(128)S(1)}, u32[]{:S(2)}) copy-start(f32[4]{0:T(128)S(1)} %multiply_divide_fusion.1) | copy-start | bytes 52
  221.3 2.5 %copy-start.3 = (bf16[2,4,128,512]{3,2,1,0:T(8,128)(2,1)S(1)}, bf16[2,4,128,512]{3,2,1,0:T(8,128)(2,1)}, u32[]{:S(2)}) copy-start(bf16[2,4,128,512]{3,2,1,0:T(8,128)(2,1)} %copy-done.2) | copy-start | bytes 3145732
  223.8 2.6 %copy-start.8 = (bf16[128,4096]{1,0:T(8,128)(2,1)S(1)}, bf16[128,4096]{1,0:T(8,128)(2,1)}, u32[]{:S(2)}) copy-start(bf16[128,4096]{1,0:T(8,128)(2,1)} %copy-done.7) | copy-start | bytes 3145732
Sparse Core Ops, SparseCore 0:
  26.1 15.7 all-gather.1

commit v3 on v2

--- a/solution.py
+++ b/solution.py
@@ -94,9 +94,10 @@
 
 def project_kernel(
     fsdp, sections, planes, chunks,
-    hidden, gain, weight, pre, feat,
-    normed, tokens, part, y_in, z_in, z_in0,
+    hidden, gain, weight, wanted, pre, feat, head,
+    normed, tokens, part, y_in, z_in, z_in0, head_in,
     tok_send, tok_recv, y_send, y_recv, z_send, z_recv, f_send, f_recv,
+    h_send, h_recv, hx_send, hx_recv, go,
 ):
     me, section = lax.axis_index("fsdp"), lax.axis_index("section")
     y, z = lax.rem(me, 2), me // 2
@@ -111,27 +112,42 @@
         r = pl.ds(pl.multiple_of(i * 16, 16), 16)
         normed[r, :] = (rms_scale(hidden[r, :].astype(F32)) * gain[...]).astype(BF)
 
-    def token_copy(j):
+    def token_copy(lane, j):
+        to = lax.rem(z + j, planes) * 2 + (1 - y if lane == 0 else y)
+        return remote(
+            normed.at[:, pl.ds(pl.multiple_of(to * depth, 128), depth)], tokens.at[y, z],
+            tok_send.at[lane, j], tok_recv.at[lane, j], fsdp=to,
+        )
+
+    share = head_in.shape[1]
+
+    def head_copy(j):
         to = lax.rem(me + j, fsdp)
         return remote(
-            normed.at[:, pl.ds(pl.multiple_of(to * depth, 128), depth)], tokens.at[y, z],
-            tok_send.at[j - 1], tok_recv.at[j - 1], fsdp=to,
-        )
-
+            wanted.at[to, pl.ds(pl.multiple_of(section * share, 16), share)], head_in.at[me],
+            h_send.at[j - 1], h_recv.at[j - 1], fsdp=to,
+        )
+
+    def head_forward(source):
+        return remote(
+            head_in, head.at[:, source], hx_send, hx_recv.at[source], section=last
+        )
+
+    for j in range(planes):
+        token_copy(0, j).start()
+    tokens[y, z] = normed[:, pl.ds(pl.multiple_of(me * depth, 128), depth)]
+    head_in[me] = wanted[me, pl.ds(pl.multiple_of(section * share, 16), share)]
+    for j in range(planes):
+        token_copy(0, j).wait_send()
+    for j in range(1, planes):
+        token_copy(1, j).start()
     for j in range(1, fsdp):
-        token_copy(j).start()
-    tokens[y, z] = normed[:, pl.ds(pl.multiple_of(me * depth, 128), depth)]
-    for j in range(1, fsdp):
-        token_copy(j).wait_recv()
+        head_copy(j).start()
+    for j in range(planes):
+        token_copy(0, j).wait_recv()
 
     def feature_copy(to):
         return remote(tokens, feat, f_send.at[to], f_recv, section=to)
-
-    @pl.when(section == last)
-    def _():
-        for to in range(last):
-            feature_copy(to).start()
-        feat[...] = tokens[...]
 
     def y_copy(c):
         return remote(
@@ -206,25 +222,60 @@
 
     ahead = min(3, chunks - 1)
 
+    def multiply(c, lane):
+        block = weight[:, pl.ds(pl.multiple_of(c * width, 128), width)]
+        part[c, lane] = (
+            jnp.dot(tokens[lane].reshape(planes * rows, depth), block, preferred_element_type=F32)
+            .astype(BF)
+            .reshape(planes, rows, width)
+        )
+
+    beside = last - 1
+
+    @pl.loop(1, chunks + 1)
+    def _(i):
+        c = lax.rem(i, chunks)
+        multiply(c, 1 - y)
+
+        @pl.when((i <= ahead) & (section != beside))
+        def _():
+            y_copy(i).start()
+
+    for j in range(1, planes):
+        token_copy(1, j).wait_recv()
+
+    @pl.when(section == last)
+    def _():
+        for to in range(last):
+            feature_copy(to).start()
+        feat[...] = tokens[...]
+
     @pl.loop(0, chunks)
     def _(c):
-        block = weight[:, pl.ds(pl.multiple_of(c * width, 128), width)]
-        for k in range(2):
-            part[c, k] = (
-                jnp.dot(
-                    tokens[k].reshape(planes * rows, depth), block, preferred_element_type=F32
-                )
-                .astype(BF)
-                .reshape(planes, rows, width)
-            )
-
-        @pl.when(c == 0)
+        multiply(c, y)
+
+        @pl.when((c == 0) & (section != beside))
         def _():
             z_start(0, 1)
 
-        @pl.when((c >= 1) & (c <= ahead))
-        def _():
-            y_copy(c).start()
+    for j in range(1, fsdp):
+        head_copy(j).wait_recv()
+
+    @pl.when(section != last)
+    def _():
+        head_forward(section).start()
+
+    @pl.when(section == last)
+    def _():
+        for f in range(fsdp):
+            head[f, last] = head_in[f]
+
+    @pl.when(section == beside)
+    def _():
+        pl.semaphore_wait(go, 1)
+        for i in range(1, ahead + 1):
+            y_copy(i).start()
+        z_start(0, 1)
 
     @pl.loop(1, chunks + planes - 1)
     def _(i):
@@ -246,6 +297,12 @@
             def _():
                 y_copy(i + ahead).start()
 
+            @pl.when((i == chunks - 2) & (section == last))
+            def _():
+                pl.semaphore_signal(
+                    go, inc=1, device_id={"section": beside}, device_id_type=MESH
+                )
+
             for d in range(planes):
                 part[i, y, d] = (part[i, y, d].astype(F32) + y_in[i, d].astype(F32)).astype(BF)
             z_start(i, 1)
@@ -276,8 +333,20 @@
         for to in range(last):
             feature_copy(to).wait_send()
 
+    @pl.when(section != last)
+    def _():
+        head[...] = jnp.zeros_like(head)
+        head_forward(section).wait_send()
+
+    @pl.when(section == last)
+    def _():
+        for source in range(last):
+            head_forward(source).wait_recv()
+
+    for j in range(1, planes):
+        token_copy(1, j).wait_send()
     for j in range(1, fsdp):
-        token_copy(j).wait_send()
+        head_copy(j).wait_send()
     y_copy0().wait_send()
     for t in range(1, planes):
         for way in range(2):
@@ -297,8 +366,9 @@
                     z_copy(c, way, t)[1].wait_send()
 
 
-def project(hidden, gain, weight, fsdp, sections):
+def project(hidden, gain, weight, wanted, fsdp, sections):
     rows, features = hidden.shape
+    share, outs = wanted.shape[1] // sections, wanted.shape[2]
     planes, chunks = fsdp // 2, CHUNKS
     depth, width = features // fsdp, features // chunks
     dma = pltpu.SemaphoreType.DMA
@@ -308,9 +378,10 @@
         out_shape=(
             jax.ShapeDtypeStruct((rows, features), BF),
             jax.ShapeDtypeStruct((2, planes, rows, depth), BF),
+            jax.ShapeDtypeStruct((fsdp, sections, share, outs), BF),
         ),
-        in_specs=[vmem] * 3,
-        out_specs=(vmem, vmem),
+        in_specs=[vmem] * 4,
+        out_specs=(vmem, vmem, vmem),
         scratch_shapes=[
             pltpu.VMEM((rows, features), BF),
             pltpu.VMEM((2, planes, rows, depth), BF),
@@ -318,14 +389,20 @@
             pltpu.VMEM((chunks, planes, rows, width), BF),
             pltpu.VMEM((chunks, 2, planes - 1, rows, width), BF),
             pltpu.VMEM((2, planes - 1, 2, rows, width), BF),
-            dma((fsdp - 1,)),
-            dma((fsdp - 1,)),
+            pltpu.VMEM((fsdp, share, outs), BF),
+            dma((2, planes)),
+            dma((2, planes)),
             dma((chunks,)),
             dma((chunks,)),
             dma((chunks, 2, planes - 1)),
             dma((chunks, 2, planes - 1)),
             dma((sections,)),
             dma,
+            dma((fsdp - 1,)),
+            dma((fsdp - 1,)),
+            dma,
+            dma((sections,)),
+            pltpu.SemaphoreType.REGULAR,
         ],
         compiler_params=pltpu.CompilerParams(
             collective_id=0, has_side_effects=True, vmem_limit_bytes=VMEM_MAX
@@ -333,12 +410,12 @@
         cost_estimate=pl.CostEstimate(
             flops=2 * fsdp * rows * depth * features, bytes_accessed=1 << 23, transcendentals=0
         ),
-    )(hidden, gain, weight)
+    )(hidden, gain, weight, wanted)
 
 
 def gather_kernel(
     fsdp, sections, planes,
-    cot, stats, cols, table,
+    tasks, cot, stats, feat, order, powers, joined, sums, weights, cols, table,
     x_send, x_recv, sx_send, sx_recv, st_send, st_recv, z_send, z_recv, y_send, y_recv,
 ):
     me, section = lax.axis_index("fsdp"), lax.axis_index("section")
@@ -405,6 +482,22 @@
 
     for j in range(1, fsdp):
         stats_f(j).start()
+
+    def add(lane, plane):
+        block = cols[lane, plane].reshape(rows, width).astype(F32)
+        row = order[pl.ds(lane * planes + plane, 1)][0]
+        scale = jnp.sum(row * weights[...], axis=1, keepdims=True)[:1]
+        block = (block * scale).astype(BF)
+        joined[...] += lax.dot_general(
+            feat[lane, plane], block, (((0,), (0,)), ((), ())), preferred_element_type=F32
+        )
+
+    def add_across(plane):
+        for h in range(HALVES):
+            y_copy(plane, h).wait_recv()
+        add(1 - y, plane)
+
+    joined[...] = jnp.zeros_like(joined)
     for h in range(HALVES):
 
         @pl.when(section != last)
@@ -418,6 +511,17 @@
                 z_copy(way, 1, h).start()
 
         y_copy(z, h).start()
+    for j in range(1, fsdp):
+        stats_f(j).wait()
+    total = jnp.sum(table[...], axis=(0, 1))
+    sums[...] = total
+    lane_number = lax.broadcasted_iota(jnp.int32, total.shape, 1)
+    counted = lane_number < tasks
+    norms = jnp.sqrt(total)
+    mean_norm = jnp.sum(jnp.where(counted, norms, 0.0), axis=1, keepdims=True) / tasks
+    ratios = jnp.where(counted, mean_norm * powers[...] / norms, 0.0)
+    weights[...] = tasks * ratios / jnp.sum(ratios, axis=1, keepdims=True)
+
     for t in range(1, planes):
         for h in range(HALVES):
             for way in range(2):
@@ -433,11 +537,30 @@
                     def _():
                         z_copy(way, t + 1, h).start()
 
-    for j in range(1, fsdp):
-        stats_f(j).wait()
+        if t == 1:
+            add(y, z)
+            add_across(z)
+        for way in range(2):
+
+            @pl.when(receives(way, t))
+            def _():
+                add(y, z - t if way == 0 else z + t)
+
+            if t > 1:
+
+                @pl.when(receives(way, t - 1))
+                def _():
+                    add_across(z - t + 1 if way == 0 else z + t - 1)
+
+    for way in range(2):
+
+        @pl.when(receives(way, planes - 1))
+        def _():
+            add_across(z - planes + 1 if way == 0 else z + planes - 1)
+
     for plane in range(planes):
         for h in range(HALVES):
-            y_copy(plane, h).wait()
+            y_copy(plane, h).wait_send()
     for t in range(1, planes):
         for h in range(HALVES):
             for way in range(2):
@@ -454,21 +577,24 @@
                 cols_x(to, h).wait_send()
 
 
-def gather(cot, stats, fsdp, sections):
+def joined_product(cot, stats, feat, order, powers, tasks, fsdp, sections):
     rows, features = cot.shape
     planes = fsdp // 2
     width = features // sections
     dma = pltpu.SemaphoreType.DMA
     vmem = pl.BlockSpec(memory_space=pltpu.VMEM)
     return pl.pallas_call(
-        functools.partial(gather_kernel, fsdp, sections, planes),
+        functools.partial(gather_kernel, fsdp, sections, planes, tasks),
         out_shape=(
-            jax.ShapeDtypeStruct((2, planes, HALVES, rows // HALVES, width), BF),
-            jax.ShapeDtypeStruct((2, planes) + stats.shape, F32),
+            jax.ShapeDtypeStruct((feat.shape[3], width), F32),
+            jax.ShapeDtypeStruct(stats.shape, F32),
+            jax.ShapeDtypeStruct(stats.shape, F32),
         ),
-        in_specs=[vmem] * 2,
-        out_specs=(vmem, vmem),
+        in_specs=[vmem] * 5,
+        out_specs=(vmem, vmem, vmem),
         scratch_shapes=[
+            pltpu.VMEM((2, planes, HALVES, rows // HALVES, width), BF),
+            pltpu.VMEM((2, planes) + stats.shape, F32),
             dma((sections, HALVES)),
             dma((HALVES,)),
             dma((sections,)),
@@ -484,15 +610,15 @@
             collective_id=1, has_side_effects=True, vmem_limit_bytes=VMEM_MAX
         ),
         cost_estimate=pl.CostEstimate(flops=0, bytes_accessed=1 << 23, transcendentals=0),
-    )(cot, stats)
-
-
-def kernels_fit(rows, features, fsdp, sections):
+    )(cot, stats, feat, order, powers)
+
+
+def kernels_fit(rows, features, fsdp, sections, head_rows, tasks):
     if fsdp < 4 or fsdp % 2 or sections < 2:
         return False
     planes = fsdp // 2
     block = rows * features * 2
-    planned = block * (2 * planes + planes + 2 * planes - 2 + 7) + features // fsdp * features * 2
+    planned = block * (2 * planes + planes + 2 * planes - 2 + 10) + features // fsdp * features * 2
     return (
         planned <= VMEM_MAX * 3 // 4
         and rows % (16 * HALVES) == 0
@@ -500,6 +626,8 @@
         and features % (128 * CHUNKS) == 0
         and features % (128 * fsdp) == 0
         and features % (128 * sections) == 0
+        and head_rows % (16 * sections) == 0
+        and 2 * tasks <= 128
         and 1 << ((fsdp.bit_length() - 1) // 2) == 2
     )
 
@@ -561,25 +689,26 @@
     hidden = activations[0]
     rows, features = hidden.shape
     weight = trunk_weight[0]
-    fused = kernels_fit(rows, features, fsdp_size, section_size)
+    fused = kernels_fit(rows, features, fsdp_size, section_size, head_rows, tasks)
+    wanted = head_weight[task_of[:, 0]]
     if fused:
-        pre, feature_all = project(hidden, norm_gain, weight, fsdp_size, section_size)
-        feature_all = feature_all.reshape(fsdp_size * rows, features // fsdp_size)
+        pre, feature_all, head_w = project(
+            hidden, norm_gain, weight, wanted, fsdp_size, section_size
+        )
     else:
         normed = (rms_scale(hidden.astype(F32)) * norm_gain[0]).astype(BF)
         feature_block = lax.all_to_all(normed, "fsdp", split_axis=1, concat_axis=0, tiled=True)
         pre = project_permuted(feature_block, weight, rows, y_size, z_size, y_place, z_place)
         feature_all = from_last(feature_block, section_index, section_size)
-
-    wanted = head_weight[task_of[:, 0]]
-    if head_rows % section_size == 0 and (head_rows // section_size) % 16 == 0:
-        share = head_rows // section_size
-        part = lax.dynamic_slice_in_dim(wanted, section_index * share, share, 1)
+        part = wanted
+        if head_rows % (16 * section_size) == 0:
+            share = head_rows // section_size
+            part = lax.dynamic_slice_in_dim(part, section_index * share, share, 1)
         part = lax.all_to_all(part, "fsdp", split_axis=0, concat_axis=0, tiled=True)
-        part = lax.all_gather(part, "section", axis=1, tiled=True)
-    else:
-        part = lax.all_to_all(wanted, "fsdp", split_axis=0, concat_axis=0, tiled=True)
-    head_w = part.reshape(features, outs)
+        if part.shape[1] != head_rows:
+            part = lax.all_gather(part, "section", axis=1, tiled=True)
+        head_w = part
+    head_w = head_w.reshape(features, outs)
 
     output = (hidden.astype(F32) + jax.nn.silu(pre.astype(F32))).astype(BF)
     passed = lax.ppermute(output, "section", [(i, i + 1) for i in range(section_size - 1)])
@@ -588,44 +717,64 @@
     onehot = (task_of[:, 0][:, None] == jnp.arange(tasks)[None, :]).astype(F32)
     counts = rows * jnp.sum(onehot, axis=0)
     own_task = (jnp.arange(tasks) == task_id).astype(F32)
-    block_loss, pullback = jax.vjp(
-        lambda inner: head_loss(
-            inner, head_w, head_mix[task_id], head_steps[task_id] + 1, targets, tasks
-        ),
-        output.astype(F32),
-    )
-    grad_out = pullback(jnp.ones_like(block_loss))[0]
-    square = jnp.sum(grad_out * grad_out)
-    pre_float = pre.astype(F32)
-    sigmoid_pre = jax.nn.sigmoid(pre_float)
-    slope_term = sigmoid_pre * (1.0 + pre_float * (1.0 - sigmoid_pre))
-    cotangent = (grad_out * slope_term).astype(BF)
-
+
+    def head_pass(output, pre, head_w):
+        block_loss, pullback = jax.vjp(
+            lambda inner: head_loss(
+                inner, head_w, head_mix[task_id], head_steps[task_id] + 1, targets, tasks
+            ),
+            output.astype(F32),
+        )
+        grad_out = pullback(jnp.ones_like(block_loss))[0]
+        square = jnp.sum(grad_out * grad_out)
+        pre_float = pre.astype(F32)
+        sigmoid_pre = jax.nn.sigmoid(pre_float)
+        slope_term = sigmoid_pre * (1.0 + pre_float * (1.0 - sigmoid_pre))
+        cotangent = (grad_out * slope_term).astype(BF)
+        return cotangent, jnp.concatenate([own_task * square, own_task * block_loss])
+
+    if fused:
+        cotangent, sums = lax.cond(
+            is_last,
+            head_pass,
+            lambda output, pre, head_w: (jnp.zeros_like(output), jnp.zeros((2 * tasks,), F32)),
+            output, pre, head_w,
+        )
+    else:
+        cotangent, sums = head_pass(output, pre, head_w)
     col_width = features // section_size
-    sums = jnp.concatenate([own_task * square, own_task * block_loss])
     if fused:
-        stats = jnp.broadcast_to(jnp.pad(sums, (0, 128 - 2 * tasks))[None, :], (8, 128))
-        column_block, table = gather(cotangent, stats, fsdp_size, section_size)
-        sums = jnp.sum(table[:, :, 0, : 2 * tasks], axis=(0, 1))
-        column_block = column_block.reshape(fsdp_size * rows, col_width)
         order = onehot.reshape(z_size, y_size, tasks).swapaxes(0, 1).reshape(fsdp_size, tasks)
-    else:
-        cols = cotangent.reshape(rows, section_size, col_width)
-        for bit in reversed(range(section_bits)):
-            half = cols.reshape(rows, 2, cols.shape[1] // 2, col_width)
-            low, high = half[:, 0], half[:, 1]
-            got = lax.ppermute(low, "section", spread_pairs(section_size, bit))
-            cols = jnp.where(section_index >> bit & 1 == 0, got, high)
-        column_block = lax.all_gather(cols[:, 0], "fsdp", axis=0, tiled=True)
-        sums = lax.psum(jnp.where(is_last, sums, jnp.zeros_like(sums)), ("section", "fsdp"))
-        order = onehot
+        order = jnp.pad(order, ((0, 0), (0, 128 - tasks)))
+        order = jnp.broadcast_to(order[:, None, :], (fsdp_size, 8, 128))
+        powers = jnp.pad(loss_ratio**ALPHA, (0, 128 - tasks), constant_values=1.0)
+        joined_grad, sums, weights = joined_product(
+            cotangent,
+            jnp.broadcast_to(jnp.pad(sums, (0, 128 - 2 * tasks))[None, :], (8, 128)),
+            feature_all,
+            order,
+            jnp.broadcast_to(powers[None, :], (8, 128)),
+            tasks,
+            fsdp_size,
+            section_size,
+        )
+        task_losses = sums[0, tasks : 2 * tasks] / (counts * outs)
+        return (passed[None], joined_grad, weights[0, :tasks], task_losses)
+    cols = cotangent.reshape(rows, section_size, col_width)
+    for bit in reversed(range(section_bits)):
+        half = cols.reshape(rows, 2, cols.shape[1] // 2, col_width)
+        low, high = half[:, 0], half[:, 1]
+        got = lax.ppermute(low, "section", spread_pairs(section_size, bit))
+        cols = jnp.where(section_index >> bit & 1 == 0, got, high)
+    column_block = lax.all_gather(cols[:, 0], "fsdp", axis=0, tiled=True)
+    sums = lax.psum(jnp.where(is_last, sums, jnp.zeros_like(sums)), ("section", "fsdp"))
     norm_sums, loss_sums = sums[:tasks], sums[tasks:]
     grad_norms = jnp.sqrt(norm_sums)
     ratios = jnp.mean(grad_norms) * loss_ratio**ALPHA / grad_norms
     task_weights = tasks * ratios / jnp.sum(ratios)
     task_losses = loss_sums / (counts * outs)
 
-    block_weight = jnp.sum(order * task_weights[None, :], axis=1)
+    block_weight = jnp.sum(onehot * task_weights[None, :], axis=1)
     scaled = (
         column_block.reshape(fsdp_size, rows, col_width).astype(F32)
         * block_weight[:, None, None]

time: 235 us -> 177 us (0.75)
  between operations: 18.2 us -> 0.83 us
  blocking collectives: 16.1 us -> 0 us
  matrix products: 9.32 us -> 0 us
  Pallas kernels: 170 us -> 161 us
  other arithmetic: 12.9 us -> 4.36 us
    all_to_all x1 -> x0, blocking collectives: 16.1 us -> none  [local(): part = lax.all_to_all(part, 'fsdp', split_axis=0, concat_axis=0, tiled=True)]
    dot_general x11 -> x0, matrix products: 9.32 us -> none  [the longest x2 4.14 us: head_loss(): outputs = jnp.dot(head_in, head_w, preferred_element_type=F32)]
    pallas_call x1, Pallas kernels: 40.9 us -> 32.5 us  [joined_product(): pl.pallas_call(functools.partial(gather_kernel, fsdp, sections, planes, t...]
    reduce_sum x6 -> x0, other arithmetic: 6.97 us -> none  [the longest x1 3.19 us: local(): square = jnp.sum(grad_out * grad_out)]
  transfers between devices with their start and end apart: 2 -> 1, of which waited for: 0 -> 0; matrix products, arithmetic and copies ran while one was open for 1% -> 2% of each run, Pallas kernels for 55% -> 18%
where the time goes in v3:
time: 177 us; the launch traced here: 176 us
  Pallas kernels  161 us (91%)
  local copies, waits for them, and re-layouts  7.77 us (4%)
  other arithmetic  4.36 us (2%)
  starting transfers between devices  2.25 us (1%)
    pallas_call x1, Pallas kernels, project(): pl.pallas_call(functools.partial(project_kernel, fsdp, sections, planes,...  129 us
    pallas_call x1, Pallas kernels, joined_product(): pl.pallas_call(functools.partial(gather_kernel, fsdp, sections, planes, t...  32.5 us
    unnamed x27, local copies, waits for them, and re-layouts  4.54 us
  transfers between devices with their start and end apart: 1, of which 0 were waited for; matrix products, arithmetic and copies ran while one was open for 2% of the time, Pallas kernels for 18%

profile of v3, /device:TPU:0, one launch (start us, length us, event | category | flops | bytes accessed | tf_op | source)
XLA Modules:
  0.0 176.3 jit_solution(13981263660331486552)
XLA Ops:
  0.6 0.0 copy-start
  0.6 0.0 copy-start.1
  0.7 0.0 copy-start.4
  0.7 0.5 broadcast.126
  1.2 1.3 fusion.79
  2.5 0.0 copy-done
  2.5 0.7 gather_fusion
  3.3 128.6 %shard_map.123 = (bf16[128,4096]{1,0:T(8,128)(2,1)S(1)}, bf16[2,4,128,512]{3,2,1,0:T(8,128)(2,1)S(1)}, bf16[8,4,128,128]{3,2,1,0:T(8,128)(2,1)}) custom-call(bf16[128,4096]{1,0:T(8,128)(2,1)S(1)} %bitcast.49, f32[1,4096]{1,0:T(1,128)S(1)} %copy-done.4, bf16[512,4096]{1,0:T(8,128)(2,1)} %bitcast.54, bf16[8,512,128]{2,1,0:T(8,128)(2,1)S(1)} %gather_fusion), custom_call_target="tpu_custom_call" | custom-call | flops 4294967296 | bytes 8388608 | tf_op jit(solution)/shard_map/pallas_call | solution.py:376
  131.9 0.0 copy-start.5
  131.9 0.0 copy-start.10
  131.9 0.0 copy-start.8
  131.9 0.0 copy-start.9
  132.0 0.0 copy-start.11
  132.0 1.6 fusion.77
  133.6 2.3 %collective-permute-start = (bf16[128,4096]{1,0:T(8,128)(2,1)}, bf16[128,4096]{1,0:T(8,128)(2,1)}, u32[]{:S(2)}, u32[]{:S(2)}) collective-permute-start(bf16[128,4096]{1,0:T(8,128)(2,1)} %fusion.77), channel_id=1, source_target_pairs={{0,8},{8,16},{16,24},{1,9},{9,17},{17,25},{2,10},{10,18},{18,26},{... | collective-permute-start | bytes 3145736 | tf_op jit(solution)/shard_map/ppermute | solution.py:714
  135.8 0.6 constant_dynamic-slice_fusion
  136.4 0.6 compare_convert_fusion
  137.1 0.1 eq.42
  137.2 0.1 copy.18
  137.3 0.1 eq.44
  137.4 0.0 copy-start.12
  137.4 1.1 conditional.1
  137.4 1.1 broadcast.62
  138.5 0.1 iota_compare_fusion
  138.6 0.4 copy-done.3
  139.0 32.5 %shard_map.124 = (f32[512,1024]{1,0:T(8,128)S(1)}, f32[8,128]{1,0:T(8,128)S(1)}, f32[8,128]{1,0:T(8,128)S(1)}) custom-call(bf16[128,4096]{1,0:T(8,128)(2,1)} %get-tuple-element.39.cot, f32[8,128]{1,0:T(8,128)S(1)} %broadcast_in_dim.14.stats, bf16[2,4,128,512]{3,2,1,0:T(8,128)(2,1)S(1)} %copy-done.3, f32[8,8,128]{2,1,0:T(8,128)S(1)} %broadcast_in_dim.15.order, ...), custom_call_target="tpu_custom_call" | custom-call | bytes 8388608 | tf_op jit(solution)/shard_map/pallas_call | solution.py:586
  171.5 0.1 convert_reduce_fusion
  171.6 0.5 slice_bitcast_fusion
  172.1 0.6 bitcast_divide_fusion
  172.7 0.0 collective-permute-done
  172.7 2.3 %copy.25 = bf16[1,128,4096]{2,1,0:T(8,128)(2,1)} copy(bf16[1,128,4096]{2,1,0:T(8,128)(2,1)} %bitcast.10) | data formatting | bytes 2097152
  175.0 1.3 copy.26
  (22 shorter events, 0.1 us)
Async XLA Ops:
  0.6 1.9 %copy-start = (bf16[4,512,128]{2,1,0:T(8,128)(2,1)S(1)}, bf16[4,512,128]{2,1,0:T(8,128)(2,1)}, u32[]{:S(2)}) copy-start(bf16[4,512,128]{2,1,0:T(8,128)(2,1)} %param.14) | copy-start | bytes 1572868
  0.6 2.6 %copy-start.1 = (bf16[1,128,4096]{2,1,0:T(8,128)(2,1)S(1)}, bf16[1,128,4096]{2,1,0:T(8,128)(2,1)}, u32[]{:S(2)}) copy-start(bf16[1,128,4096]{2,1,0:T(8,128)(2,1)} %param.11) | copy-start | bytes 3145732
  0.7 2.6 %copy-start.4 = (f32[1,4096]{1,0:T(1,128)S(1)}, f32[1,4096]{1,0:T(1,128)}, u32[]{:S(2)}) copy-start(f32[1,4096]{1,0:T(1,128)} %gain.1) | copy-start | bytes 49156
  131.9 1.7 copy-start.2
  131.9 3.9 %copy-start.5 = (bf16[128,4096]{1,0:T(8,128)(2,1)}, bf16[128,4096]{1,0:T(8,128)(2,1)S(1)}, u32[]{:S(2)}) copy-start(bf16[128,4096]{1,0:T(8,128)(2,1)S(1)} %get-tuple-element.37) | copy-start | bytes 3145732
  131.9 3.9 %copy-start.10 = (s32[8,1]{0,1:T(1,128)S(1)}, s32[8,1]{0,1:T(1,128)}, u32[]{:S(2)}) copy-start(s32[8,1]{0,1:T(1,128)} %param.17) | copy-start | bytes 100
  131.9 5.4 %copy-start.7 = (bf16[8,4,128,128]{3,2,1,0:T(8,128)(2,1)S(1)}, bf16[8,4,128,128]{3,2,1,0:T(8,128)(2,1)}, u32[]{:S(2)}) copy-start(bf16[8,4,128,128]{3,2,1,0:T(8,128)(2,1)} %get-tuple-element.38) | copy-start | bytes 3145732
  131.9 5.4 %copy-start.8 = (f32[4,128,128]{2,1,0:T(8,128)S(1)}, f32[4,128,128]{2,1,0:T(8,128)}, u32[]{:S(2)}) copy-start(f32[4,128,128]{2,1,0:T(8,128)} %param.15) | copy-start | bytes 786436
  131.9 5.4 %copy-start.9 = (bf16[128,128]{1,0:T(8,128)(2,1)S(1)}, bf16[128,128]{1,0:T(8,128)(2,1)}, u32[]{:S(2)}) copy-start(bf16[128,128]{1,0:T(8,128)(2,1)} %param.19) | copy-start | bytes 98308
  132.0 5.4 %copy-start.11 = (s32[4]{0:T(128)S(1)}, s32[4]{0:T(128)}, u32[]{:S(2)}) copy-start(s32[4]{0:T(128)} %param.16) | copy-start | bytes 52
  133.6 39.1 %collective-permute-start = (bf16[128,4096]{1,0:T(8,128)(2,1)}, bf16[128,4096]{1,0:T(8,128)(2,1)}, u32[]{:S(2)}, u32[]{:S(2)}) collective-permute-start(bf16[128,4096]{1,0:T(8,128)(2,1)} %fusion.77), channel_id=1, source_target_pairs={{0,8},{8,16},{16,24},{1,9},{9,17},{17,25},{2,10},{10,18},{18,26},{... | collective-permute-start | bytes 3145736 | tf_op jit(solution)/shard_map/ppermute | solution.py:714
  137.4 1.1 copy-start.12
  137.4 1.6 copy-start.3

commit v4 on v3

--- a/solution.py
+++ b/solution.py
@@ -94,7 +94,7 @@
 
 def project_kernel(
     fsdp, sections, planes, chunks,
-    hidden, gain, weight, wanted, pre, feat, head,
+    hidden, gain, weight, wanted, pre, out, feat, head,
     normed, tokens, part, y_in, z_in, z_in0, head_in,
     tok_send, tok_recv, y_send, y_recv, z_send, z_recv, f_send, f_recv,
     h_send, h_recv, hx_send, hx_recv, go,
@@ -143,9 +143,6 @@
         token_copy(1, j).start()
     for j in range(1, fsdp):
         head_copy(j).start()
-    for j in range(planes):
-        token_copy(0, j).wait_recv()
-
     def feature_copy(to):
         return remote(tokens, feat, f_send.at[to], f_recv, section=to)
 
@@ -230,16 +227,37 @@
             .reshape(planes, rows, width)
         )
 
+    def finish(c, value):
+        columns = pl.ds(pl.multiple_of(c * width, 128), width)
+        pre[:, columns] = value
+        wide = value.astype(F32)
+        out[:, columns] = (
+            hidden[:, columns].astype(F32) + wide * jax.nn.sigmoid(wide)
+        ).astype(BF)
+
     beside = last - 1
 
-    @pl.loop(1, chunks + 1)
+    for j in range(planes):
+        token_copy(0, j).wait_recv()
+        d = lax.rem(z + planes - j, planes)
+
+        @pl.loop(1, ahead + 1)
+        def _(c):
+            block = weight[:, pl.ds(pl.multiple_of(c * width, 128), width)]
+            part[c, 1 - y, d] = jnp.dot(
+                tokens[1 - y, d], block, preferred_element_type=F32
+            ).astype(BF)
+
+            @pl.when(section != beside)
+            def _():
+                remote(
+                    part.at[c, 1 - y, d], y_in.at[c, d], y_send.at[c], y_recv.at[c],
+                    fsdp=z * 2 + 1 - y,
+                ).start()
+
+    @pl.loop(ahead + 1, chunks + 1)
     def _(i):
-        c = lax.rem(i, chunks)
-        multiply(c, 1 - y)
-
-        @pl.when((i <= ahead) & (section != beside))
-        def _():
-            y_copy(i).start()
+        multiply(lax.rem(i, chunks), 1 - y)
 
     for j in range(1, planes):
         token_copy(1, j).wait_recv()
@@ -319,10 +337,10 @@
         @pl.when((c >= 1) & (c < chunks))
         def _():
             z_last(c)
-            pre[:, pl.ds(pl.multiple_of(c * width, 128), width)] = part[c, y, z]
+            finish(c, part[c, y, z])
 
     y_copy0().wait_recv()
-    pre[:, pl.ds(0, width)] = (part[0, y, z].astype(F32) + y_in[0, 0].astype(F32)).astype(BF)
+    finish(0, (part[0, y, z].astype(F32) + y_in[0, 0].astype(F32)).astype(BF))
 
     @pl.when(section != last)
     def _():
@@ -377,11 +395,12 @@
         functools.partial(project_kernel, fsdp, sections, planes, chunks),
         out_shape=(
             jax.ShapeDtypeStruct((rows, features), BF),
+            jax.ShapeDtypeStruct((rows, features), BF),
             jax.ShapeDtypeStruct((2, planes, rows, depth), BF),
             jax.ShapeDtypeStruct((fsdp, sections, share, outs), BF),
         ),
         in_specs=[vmem] * 4,
-        out_specs=(vmem, vmem, vmem),
+        out_specs=(vmem,) * 4,
         scratch_shapes=[
             pltpu.VMEM((rows, features), BF),
             pltpu.VMEM((2, planes, rows, depth), BF),
@@ -415,8 +434,9 @@
 
 def gather_kernel(
     fsdp, sections, planes,
-    tasks, cot, stats, feat, order, powers, joined, sums, weights, cols, table,
+    tasks, cot, stats, feat, order, powers, out, joined, sums, weights, passed, cols, table,
     x_send, x_recv, sx_send, sx_recv, st_send, st_recv, z_send, z_recv, y_send, y_recv,
+    p_send, p_recv,
 ):
     me, section = lax.axis_index("fsdp"), lax.axis_index("section")
     y, z = lax.rem(me, 2), me // 2
@@ -426,6 +446,9 @@
     size = rows // HALVES
     greet(fsdp, sections)
 
+    def pass_copy():
+        return remote(out, passed, p_send, p_recv, section=lax.rem(section + 1, sections))
+
     def stats_x(to):
         return remote(stats, table.at[y, z], sx_send.at[to], sx_recv, section=to)
 
@@ -482,6 +505,14 @@
 
     for j in range(1, fsdp):
         stats_f(j).start()
+
+    @pl.when(section != last)
+    def _():
+        pass_copy().start()
+
+    @pl.when(section == 0)
+    def _():
+        passed[...] = jnp.zeros_like(passed)
 
     def add(lane, plane):
         block = cols[lane, plane].reshape(rows, width).astype(F32)
@@ -558,6 +589,14 @@
         def _():
             add_across(z - planes + 1 if way == 0 else z + planes - 1)
 
+    @pl.when(section != 0)
+    def _():
+        pass_copy().wait_recv()
+
+    @pl.when(section != last)
+    def _():
+        pass_copy().wait_send()
+
     for plane in range(planes):
         for h in range(HALVES):
             y_copy(plane, h).wait_send()
@@ -577,7 +616,7 @@
                 cols_x(to, h).wait_send()
 
 
-def joined_product(cot, stats, feat, order, powers, tasks, fsdp, sections):
+def joined_product(cot, stats, feat, order, powers, out, tasks, fsdp, sections):
     rows, features = cot.shape
     planes = fsdp // 2
     width = features // sections
@@ -589,9 +628,10 @@
             jax.ShapeDtypeStruct((feat.shape[3], width), F32),
             jax.ShapeDtypeStruct(stats.shape, F32),
             jax.ShapeDtypeStruct(stats.shape, F32),
+            jax.ShapeDtypeStruct(out.shape, BF),
         ),
-        in_specs=[vmem] * 5,
-        out_specs=(vmem, vmem, vmem),
+        in_specs=[vmem] * 6,
+        out_specs=(vmem,) * 4,
         scratch_shapes=[
             pltpu.VMEM((2, planes, HALVES, rows // HALVES, width), BF),
             pltpu.VMEM((2, planes) + stats.shape, F32),
@@ -605,12 +645,14 @@
             dma((2, planes - 1, HALVES)),
             dma((planes, HALVES)),
             dma((planes, HALVES)),
+            dma,
+            dma,
         ],
         compiler_params=pltpu.CompilerParams(
             collective_id=1, has_side_effects=True, vmem_limit_bytes=VMEM_MAX
         ),
         cost_estimate=pl.CostEstimate(flops=0, bytes_accessed=1 << 23, transcendentals=0),
-    )(cot, stats, feat, order, powers)
+    )(cot, stats, feat, order, powers, out)
 
 
 def kernels_fit(rows, features, fsdp, sections, head_rows, tasks):
@@ -692,7 +734,7 @@
     fused = kernels_fit(rows, features, fsdp_size, section_size, head_rows, tasks)
     wanted = head_weight[task_of[:, 0]]
     if fused:
-        pre, feature_all, head_w = project(
+        pre, output, feature_all, head_w = project(
             hidden, norm_gain, weight, wanted, fsdp_size, section_size
         )
     else:
@@ -710,8 +752,9 @@
         head_w = part
     head_w = head_w.reshape(features, outs)
 
-    output = (hidden.astype(F32) + jax.nn.silu(pre.astype(F32))).astype(BF)
-    passed = lax.ppermute(output, "section", [(i, i + 1) for i in range(section_size - 1)])
+    if not fused:
+        output = (hidden.astype(F32) + jax.nn.silu(pre.astype(F32))).astype(BF)
+        passed = lax.ppermute(output, "section", [(i, i + 1) for i in range(section_size - 1)])
 
     task_id = task_of[member, 0]
     onehot = (task_of[:, 0][:, None] == jnp.arange(tasks)[None, :]).astype(F32)
@@ -748,12 +791,13 @@
         order = jnp.pad(order, ((0, 0), (0, 128 - tasks)))
         order = jnp.broadcast_to(order[:, None, :], (fsdp_size, 8, 128))
         powers = jnp.pad(loss_ratio**ALPHA, (0, 128 - tasks), constant_values=1.0)
-        joined_grad, sums, weights = joined_product(
+        joined_grad, sums, weights, passed = joined_product(
             cotangent,
             jnp.broadcast_to(jnp.pad(sums, (0, 128 - 2 * tasks))[None, :], (8, 128)),
             feature_all,
             order,
             jnp.broadcast_to(powers[None, :], (8, 128)),
+            output,
             tasks,
             fsdp_size,
             section_size,

time: 177 us -> 172 us (0.972)
  starting transfers between devices: 2.25 us -> 0 us
    ppermute x1 -> x0, starting transfers between devices: 2.25 us -> none  [local(): lax.ppermute(output, 'section', [(i, i + 1) for i in range(section_size -...]
    unnamed x27 -> x19, local copies, waits for them, and re-layouts: 4.54 us -> 4.06 us
  transfers between devices with their start and end apart: 1 -> 0, of which waited for: 0 -> 0; matrix products, arithmetic and copies ran while one was open for 2% -> 0% of each run, Pallas kernels for 18% -> 0%
where the time goes in v4:
time: 172 us
  Pallas kernels  160 us (93%)
  local copies, waits for them, and re-layouts  7.98 us (5%)
  other arithmetic  2.76 us (2%)
    pallas_call x1, Pallas kernels, project(): pl.pallas_call(functools.partial(project_kernel, fsdp, sections, planes,...  129 us
    pallas_call x1, Pallas kernels, joined_product(): pl.pallas_call(functools.partial(gather_kernel, fsdp, sections, planes, t...  31.1 us
    unnamed x19, local copies, waits for them, and re-layouts  4.06 us

profile of v4, /device:TPU:0, one launch (start us, length us, event | category | flops | bytes accessed | tf_op | source)
XLA Modules:
  0.0 171.9 jit_solution(1005806707764035674)
XLA Ops:
  0.6 0.0 copy-start
  0.6 0.0 copy-start.2
  0.7 1.3 constant_dynamic-slice_fusion
  2.0 0.6 compare_convert_fusion
  2.6 0.5 broadcast.124
  3.1 1.3 fusion.74
  4.5 0.0 copy-done
  4.5 0.7 gather_fusion
  5.2 0.0 copy-done.2
  5.2 0.0 copy-start.1
  5.2 1.2 copy-done.1
  6.5 0.0 copy-start.5
  6.5 0.0 copy-start.7
  6.5 129.2 %shard_map.123 = (bf16[128,4096]{1,0:T(8,128)(2,1)}, bf16[128,4096]{1,0:T(8,128)(2,1)}, bf16[2,4,128,512]{3,2,1,0:T(8,128)(2,1)S(1)}, bf16[8,4,128,128]{3,2,1,0:T(8,128)(2,1)}) custom-call(bf16[128,4096]{1,0:T(8,128)(2,1)S(1)} %bitcast.49, f32[1,4096]{1,0:T(1,128)S(1)} %copy-done.2, bf16[512,4096]{1,0:T(8,128)(2,1)} %bitcast.54, ...), custom_call_target="tpu_custom_call" | custom-call | flops 4294967296 | bytes 8388608 | tf_op jit(solution)/shard_map/pallas_call | solution.py:394
  135.7 0.0 copy-done.5
  135.7 0.0 copy-done.7
  135.7 0.0 copy-done.9
  135.7 0.0 copy-start.10
  135.7 1.1 conditional.1
  135.8 1.1 broadcast.60
  136.9 0.1 eq.42
  136.9 0.1 copy.18
  137.0 0.1 eq.44
  137.1 0.1 iota_compare_fusion
  137.2 0.0 copy-done.10
  137.3 31.1 %shard_map.124 = (f32[512,1024]{1,0:T(8,128)S(1)}, f32[8,128]{1,0:T(8,128)S(1)}, f32[8,128]{1,0:T(8,128)S(1)}, bf16[128,4096]{1,0:T(8,128)(2,1)S(1)}) custom-call(bf16[128,4096]{1,0:T(8,128)(2,1)} %get-tuple-element.42.cot, f32[8,128]{1,0:T(8,128)S(1)} %broadcast_in_dim.13.stats, bf16[2,4,128,512]{3,2,1,0:T(8,128)(2,1)S(1)} %get-tuple-element.44.feat, ...), custom_call_target="tpu_custom_call" | custom-call | bytes 8388608 | tf_op jit(solution)/shard_map/pallas_call | solution.py:625
  168.4 0.0 copy-done.8
  168.4 0.1 convert_reduce_fusion
  168.5 0.6 bitcast_divide_fusion
  169.1 0.5 slice_bitcast_fusion
  169.6 1.0 copy.25
  170.6 1.3 copy.26
  (11 shorter events, 0.0 us)
Async XLA Ops:
  0.6 3.8 %copy-start = (bf16[4,512,128]{2,1,0:T(8,128)(2,1)S(1)}, bf16[4,512,128]{2,1,0:T(8,128)(2,1)}, u32[]{:S(2)}) copy-start(bf16[4,512,128]{2,1,0:T(8,128)(2,1)} %param.14) | copy-start | bytes 1572868
  0.6 4.6 %copy-start.2 = (f32[1,4096]{1,0:T(1,128)S(1)}, f32[1,4096]{1,0:T(1,128)}, u32[]{:S(2)}) copy-start(f32[1,4096]{1,0:T(1,128)} %gain.1) | copy-start | bytes 49156
  5.2 1.2 copy-start.1
  6.5 129.2 %copy-start.5 = (f32[4,128,128]{2,1,0:T(8,128)S(1)}, f32[4,128,128]{2,1,0:T(8,128)}, u32[]{:S(2)}) copy-start(f32[4,128,128]{2,1,0:T(8,128)} %param.15) | copy-start | bytes 786436
  6.5 129.3 %copy-start.7 = (bf16[128,128]{1,0:T(8,128)(2,1)S(1)}, bf16[128,128]{1,0:T(8,128)(2,1)}, u32[]{:S(2)}) copy-start(bf16[128,128]{1,0:T(8,128)(2,1)} %param.19) | copy-start | bytes 98308
  6.5 129.3 %copy-start.9 = (s32[4]{0:T(128)S(1)}, s32[4]{0:T(128)}, u32[]{:S(2)}) copy-start(s32[4]{0:T(128)} %param.16) | copy-start | bytes 52
  135.7 1.5 copy-start.10
  136.8 31.6 %copy-start.8 = (s32[8,1]{0,1:T(1,128)S(1)}, s32[8,1]{0,1:T(1,128)}, u32[]{:S(2)}) copy-start(s32[8,1]{0,1:T(1,128)} %param.17) | copy-start | bytes 100

commit v5 on v4

--- a/solution.py
+++ b/solution.py
@@ -255,10 +255,6 @@
                     fsdp=z * 2 + 1 - y,
                 ).start()
 
-    @pl.loop(ahead + 1, chunks + 1)
-    def _(i):
-        multiply(lax.rem(i, chunks), 1 - y)
-
     for j in range(1, planes):
         token_copy(1, j).wait_recv()
 
@@ -268,28 +264,31 @@
             feature_copy(to).start()
         feat[...] = tokens[...]
 
-    @pl.loop(0, chunks)
-    def _(c):
-        multiply(c, y)
-
-        @pl.when((c == 0) & (section != beside))
+    multiply(0, 1 - y)
+    multiply(0, y)
+
+    @pl.when(section != beside)
+    def _():
+        z_start(0, 1)
+
+    multiply(1, y)
+
+    def share_head():
+        for j in range(1, fsdp):
+            head_copy(j).wait_recv()
+
+        @pl.when(section != last)
         def _():
-            z_start(0, 1)
-
-    for j in range(1, fsdp):
-        head_copy(j).wait_recv()
-
-    @pl.when(section != last)
-    def _():
-        head_forward(section).start()
-
-    @pl.when(section == last)
-    def _():
-        for f in range(fsdp):
-            head[f, last] = head_in[f]
+            head_forward(section).start()
+
+        @pl.when(section == last)
+        def _():
+            for f in range(fsdp):
+                head[f, last] = head_in[f]
 
     @pl.when(section == beside)
     def _():
+        share_head()
         pl.semaphore_wait(go, 1)
         for i in range(1, ahead + 1):
             y_copy(i).start()
@@ -297,6 +296,42 @@
 
     @pl.loop(1, chunks + planes - 1)
     def _(i):
+        @pl.when(i + ahead < chunks)
+        def _():
+            multiply(i + ahead, 1 - y)
+
+        @pl.when(i < chunks)
+        def _():
+            y_copy(i).wait_recv()
+
+            @pl.when(i + ahead < chunks)
+            def _():
+                y_copy(i + ahead).start()
+
+            @pl.when((i == chunks - 2) & (section == last))
+            def _():
+                pl.semaphore_signal(
+                    go, inc=1, device_id={"section": beside}, device_id_type=MESH
+                )
+
+            for d in range(planes):
+                part[i, y, d] = (part[i, y, d].astype(F32) + y_in[i, d].astype(F32)).astype(BF)
+            z_start(i, 1)
+
+        for t in range(1, planes - 1):
+            c = i - t
+
+            @pl.when((c >= 1) & (c < chunks))
+            def _():
+                z_start(c, t + 1)
+
+        c = i - (planes - 1)
+
+        @pl.when((c >= 1) & (c < chunks))
+        def _():
+            z_last(c)
+            finish(c, part[c, y, z])
+
         for t in range(1, planes):
 
             @pl.when(i == t)
@@ -307,37 +342,13 @@
                     z_last(0)
                     y_copy0().start()
 
-        @pl.when(i < chunks)
+        @pl.when((i == 2) & (section != beside))
         def _():
-            y_copy(i).wait_recv()
-
-            @pl.when(i + ahead < chunks)
-            def _():
-                y_copy(i + ahead).start()
-
-            @pl.when((i == chunks - 2) & (section == last))
-            def _():
-                pl.semaphore_signal(
-                    go, inc=1, device_id={"section": beside}, device_id_type=MESH
-                )
-
-            for d in range(planes):
-                part[i, y, d] = (part[i, y, d].astype(F32) + y_in[i, d].astype(F32)).astype(BF)
-            z_start(i, 1)
-
-        for t in range(1, planes - 1):
-            c = i - t
-
-            @pl.when((c >= 1) & (c < chunks))
-            def _():
-                z_start(c, t + 1)
-
-        c = i - (planes - 1)
-
-        @pl.when((c >= 1) & (c < chunks))
+            share_head()
+
+        @pl.when(i + 1 < chunks)
         def _():
-            z_last(c)
-            finish(c, part[c, y, z])
+            multiply(i + 1, y)
 
     y_copy0().wait_recv()
     finish(0, (part[0, y, z].astype(F32) + y_in[0, 0].astype(F32)).astype(BF))

time: 172 us -> 172 us (level)
  no operation moved by 1% of the time
where the time goes in v5:
time: 172 us
  Pallas kernels  160 us (93%)
  local copies, waits for them, and re-layouts  7.98 us (5%)
  other arithmetic  2.76 us (2%)
    pallas_call x1, Pallas kernels, project(): pl.pallas_call(functools.partial(project_kernel, fsdp, sections, planes,...  129 us
    pallas_call x1, Pallas kernels, joined_product(): pl.pallas_call(functools.partial(gather_kernel, fsdp, sections, planes, t...  31.1 us
    unnamed x19, local copies, waits for them, and re-layouts  4.06 us

profile of v5, /device:TPU:0, one launch (start us, length us, event | category | flops | bytes accessed | tf_op | source)
XLA Modules:
  0.0 171.9 jit_solution(18183763962681935266)
XLA Ops:
  0.6 0.0 copy-start
  0.6 0.0 copy-start.2
  0.7 1.3 constant_dynamic-slice_fusion
  2.0 0.6 compare_convert_fusion
  2.6 0.5 broadcast.124
  3.1 1.3 fusion.74
  4.5 0.0 copy-done
  4.5 0.7 gather_fusion
  5.2 0.0 copy-done.2
  5.2 0.0 copy-start.1
  5.2 1.2 copy-done.1
  6.5 0.0 copy-start.5
  6.5 0.0 copy-start.7
  6.5 129.3 %shard_map.123 = (bf16[128,4096]{1,0:T(8,128)(2,1)}, bf16[128,4096]{1,0:T(8,128)(2,1)}, bf16[2,4,128,512]{3,2,1,0:T(8,128)(2,1)S(1)}, bf16[8,4,128,128]{3,2,1,0:T(8,128)(2,1)}) custom-call(bf16[128,4096]{1,0:T(8,128)(2,1)S(1)} %bitcast.49, f32[1,4096]{1,0:T(1,128)S(1)} %copy-done.2, bf16[512,4096]{1,0:T(8,128)(2,1)} %bitcast.54, ...), custom_call_target="tpu_custom_call" | custom-call | flops 4294967296 | bytes 8388608 | tf_op jit(solution)/shard_map/pallas_call | solution.py:405
  135.7 0.0 copy-done.5
  135.7 0.0 copy-done.7
  135.8 0.0 copy-done.9
  135.8 0.0 copy-start.10
  135.8 1.1 conditional.1
  135.8 1.1 broadcast.60
  136.9 0.1 eq.42
  137.0 0.1 copy.18
  137.1 0.1 eq.44
  137.1 0.1 iota_compare_fusion
  137.2 0.0 copy-done.10
  137.3 31.1 %shard_map.124 = (f32[512,1024]{1,0:T(8,128)S(1)}, f32[8,128]{1,0:T(8,128)S(1)}, f32[8,128]{1,0:T(8,128)S(1)}, bf16[128,4096]{1,0:T(8,128)(2,1)S(1)}) custom-call(bf16[128,4096]{1,0:T(8,128)(2,1)} %get-tuple-element.42.cot, f32[8,128]{1,0:T(8,128)S(1)} %broadcast_in_dim.13.stats, bf16[2,4,128,512]{3,2,1,0:T(8,128)(2,1)S(1)} %get-tuple-element.44.feat, ...), custom_call_target="tpu_custom_call" | custom-call | bytes 8388608 | tf_op jit(solution)/shard_map/pallas_call | solution.py:636
  168.4 0.0 copy-done.8
  168.4 0.1 convert_reduce_fusion
  168.6 0.6 bitcast_divide_fusion
  169.1 0.5 slice_bitcast_fusion
  169.7 1.0 copy.25
  170.6 1.3 copy.26
  (11 shorter events, 0.0 us)
Async XLA Ops:
  0.6 3.8 %copy-start = (bf16[4,512,128]{2,1,0:T(8,128)(2,1)S(1)}, bf16[4,512,128]{2,1,0:T(8,128)(2,1)}, u32[]{:S(2)}) copy-start(bf16[4,512,128]{2,1,0:T(8,128)(2,1)} %param.14) | copy-start | bytes 1572868
  0.6 4.6 %copy-start.2 = (f32[1,4096]{1,0:T(1,128)S(1)}, f32[1,4096]{1,0:T(1,128)}, u32[]{:S(2)}) copy-start(f32[1,4096]{1,0:T(1,128)} %gain.1) | copy-start | bytes 49156
  5.2 1.2 copy-start.1
  6.5 129.3 %copy-start.5 = (f32[4,128,128]{2,1,0:T(8,128)S(1)}, f32[4,128,128]{2,1,0:T(8,128)}, u32[]{:S(2)}) copy-start(f32[4,128,128]{2,1,0:T(8,128)} %param.15) | copy-start | bytes 786436
  6.5 129.3 %copy-start.7 = (bf16[128,128]{1,0:T(8,128)(2,1)S(1)}, bf16[128,128]{1,0:T(8,128)(2,1)}, u32[]{:S(2)}) copy-start(bf16[128,128]{1,0:T(8,128)(2,1)} %param.19) | copy-start | bytes 98308
  6.5 129.3 %copy-start.9 = (s32[4]{0:T(128)S(1)}, s32[4]{0:T(128)}, u32[]{:S(2)}) copy-start(s32[4]{0:T(128)} %param.16) | copy-start | bytes 52
  135.8 1.5 copy-start.10
  136.9 31.6 %copy-start.8 = (s32[8,1]{0,1:T(1,128)S(1)}, s32[8,1]{0,1:T(1,128)}, u32[]{:S(2)}) copy-start(s32[8,1]{0,1:T(1,128)} %param.17) | copy-start | bytes 100
